TPU v7x, 32 devices: a whole 2x2x4 slice. The times are simulated.
32 devices in a mesh: ctx: 16 (over z, x, core), dp: 2 (over y).
Axes of the slice: x: 2, y: 2, z: 4, core: 2. Of those that a mesh axis runs over, the one named last changes fastest.
Arguments:
- hidden_in: bfloat16 [2048, 2048], P('ctx'), may hold values from -6 to 6
- query_vectors: bfloat16 [2048, 1024], P('ctx', 'dp'), may hold values from -6 to 6
- key_vectors: bfloat16 [2048, 1024], P('ctx', 'dp')
- value_vectors: bfloat16 [2048, 2048], P('ctx', 'dp'), may hold values from -6 to 6
- out_cotangent: bfloat16 [2048, 2048], P('ctx', 'dp'), may hold values from -6 to 6
- w_decay: bfloat16 [2048, 16], P(None, 'dp'), may hold values from -0.125 to 0.125
- w_beta: bfloat16 [2048, 16], P(None, 'dp'), may hold values from -0.125 to 0.125
- log_decay_rate: float32 [16], P('dp')
- step_bias: float32 [16], P('dp'), may hold values from -1 to 1
- doc_start: int32 [1], replicated, may hold values from 0 to 2047
Outputs:
- query_grad: bfloat16 [2048, 1024], P('ctx', 'dp')
- key_grad: bfloat16 [2048, 1024], P('ctx', 'dp')
- value_grad: bfloat16 [2048, 2048], P('ctx', 'dp')
- hidden_grad: bfloat16 [2048, 2048], P('ctx', 'dp')
- w_decay_grad: float32 [2048, 16], P(None, 'dp')
- w_beta_grad: float32 [2048, 16], P(None, 'dp')
- rate_grad: float32 [16], P('dp')
- bias_grad: float32 [16], P('dp')
Inputs may be any that keep to these rules, and one draw needn't show every extreme that they name: `doc_start`: the state is cleared at that position.
All inputs are finite; a program needn't handle non-finite values.
Results may differ from a plain program's by a relative error of at most 0.0024.
Values may be sent and summed in bfloat16 or wider, within the bound.
A program may use at most 128 MiB of HBM per device.

v0:
```python
import jax
import jax.numpy as jnp
from jax import lax
from jax.sharding import PartitionSpec as P

DK = 128
DV = 128
BLOCK = 64


norm_epsilon = 1e-06


def entering(part, axis, combine, identity, reverse):
    count = lax.axis_size(axis)
    place = lax.axis_index(axis)
    ahead = count - 1 - place if reverse else place
    gathered = jax.tree.map(lambda a: lax.all_gather(a, axis), part)
    state = jax.tree.map(lambda a, e: jnp.zeros_like(a) + jnp.asarray(e, a.dtype), part, identity)

    def one(step, state):
        source = count - 1 - step if reverse else step
        return combine(
            state, jax.tree.map(lambda a: lax.dynamic_index_in_dim(a, source, 0, False), gathered)
        )

    return lax.fori_loop(0, ahead, one, state)


def unit_rows(source):
    return source * lax.rsqrt(jnp.sum(source * source, axis=-1, keepdims=True) + norm_epsilon)


def block_step(carried, pieces):
    query_block, key_block, value_block, decay_block, beta_block, reset_block = pieces
    length = query_block.shape[-2]
    highest = lax.Precision.HIGHEST
    cumulative = jnp.cumsum(decay_block, axis=-1)
    counted = jnp.cumsum(reset_block, axis=-1)
    places = jnp.arange(length, dtype=jnp.int32)
    lower_mask = places[:, None] >= places[None, :]
    strict_mask = places[:, None] > places[None, :]
    same_doc = (counted[:, :, None] == counted[:, None, :])[:, None]
    keep_mask = jnp.logical_and(lower_mask, same_doc)
    spread = cumulative[..., :, None] - cumulative[..., None, :]
    decay_matrix = jnp.where(keep_mask, jnp.exp(jnp.where(keep_mask, spread, 0.0)), 0.0)
    carry_in = jnp.where(counted[:, None, :] == 0, jnp.exp(cumulative), 0.0)
    key_gram = jnp.einsum("bhid,bhjd->bhij", key_block, key_block, precision=highest)
    coupling = jnp.where(strict_mask, beta_block[..., :, None] * decay_matrix * key_gram, 0.0)
    key_state = jnp.einsum("bhid,bhde->bhie", key_block, carried, precision=highest)
    target = beta_block[..., None] * (value_block - carry_in[..., None] * key_state)
    system = coupling + jnp.eye(length, dtype=jnp.float32)
    updates = lax.linalg.triangular_solve(
        system, target, left_side=True, lower=True, unit_diagonal=True
    )
    query_key = jnp.einsum("bhid,bhjd->bhij", query_block, key_block, precision=highest)
    from_state = jnp.einsum("bhid,bhde->bhie", query_block, carried, precision=highest)
    outputs = carry_in[..., None] * from_state + jnp.einsum(
        "bhij,bhje->bhie", query_key * decay_matrix, updates, precision=highest
    )
    weighted_keys = key_block * decay_matrix[..., -1, :, None]
    new_state = carry_in[..., -1, None, None] * carried + jnp.einsum(
        "bhjd,bhje->bhde", weighted_keys, updates, precision=highest
    )
    return (new_state, outputs)


def blocked(source, blocks):
    seq_count, tokens = (source.shape[0], source.shape[1])
    shaped = source.reshape((seq_count, blocks, tokens // blocks) + source.shape[2:])
    if source.ndim == 4:
        return shaped.transpose(1, 0, 3, 2, 4)
    if source.ndim == 3:
        return shaped.transpose(1, 0, 3, 2)
    return shaped.transpose(1, 0, 2)


def run_block(carried, queries_f, keys_f, values_f, logit_rows, rate_logs, biases, resets):
    seq_count, tokens = (logit_rows.shape[0], logit_rows.shape[1])
    head_count = rate_logs.shape[0]
    size_key = carried.shape[2]
    size_value = carried.shape[3]
    group_size = head_count // (queries_f.shape[2] // size_key)
    log_decay = -jnp.exp(rate_logs) * jax.nn.softplus(logit_rows[..., :head_count] + biases)
    beta_all = jax.nn.sigmoid(logit_rows[..., head_count:])
    query_heads = unit_rows(queries_f.reshape(seq_count, tokens, -1, size_key)) * size_key ** (-0.5)
    key_heads = unit_rows(keys_f.reshape(seq_count, tokens, -1, size_key))
    query_heads = jnp.repeat(query_heads, group_size, axis=2)
    key_heads = jnp.repeat(key_heads, group_size, axis=2)
    value_heads = values_f.reshape(seq_count, tokens, head_count, size_value)
    blocks = tokens // BLOCK
    pieces = (
        blocked(query_heads, blocks),
        blocked(key_heads, blocks),
        blocked(value_heads, blocks),
        blocked(log_decay, blocks),
        blocked(beta_all, blocks),
        blocked(resets, blocks),
    )
    final_state, outputs = lax.scan(jax.checkpoint(block_step), carried, pieces)
    outputs = outputs.transpose(1, 0, 3, 2, 4).reshape(seq_count, tokens, head_count * size_value)
    return (outputs, final_state)


def apply_map(matrices, incoming):
    return jnp.einsum("bhij,bhjk->bhik", matrices, incoming, precision=lax.Precision.HIGHEST)


def compose(earlier, following):
    return (apply_map(following[0], earlier[0]), apply_map(following[0], earlier[1]) + following[1])


def on_device(
    hidden_in,
    query_vectors,
    key_vectors,
    value_vectors,
    out_cotangent,
    w_decay,
    w_beta,
    log_decay_rate,
    step_bias,
    doc_start,
):
    tokens = hidden_in.shape[0]
    head_count = log_decay_rate.shape[0]
    highest = lax.Precision.HIGHEST
    both_weights = jnp.concatenate([w_decay, w_beta], axis=1)
    logits = jnp.dot(hidden_in, both_weights, preferred_element_type=jnp.float32)[None]
    offset = lax.axis_index("ctx") * tokens
    positions = offset + jnp.arange(tokens, dtype=jnp.int32)
    resets = (positions == doc_start[0]).astype(jnp.float32)[None]
    query_f = query_vectors.astype(jnp.float32)[None]
    key_f = key_vectors.astype(jnp.float32)[None]
    value_f = value_vectors.astype(jnp.float32)[None]
    cotangent = out_cotangent.astype(jnp.float32)[None]
    zero_state = jnp.zeros((1, head_count, DK, DV), jnp.float32)
    identity = jnp.broadcast_to(jnp.eye(DK, dtype=jnp.float32), zero_state.shape)

    def from_state(carried):
        return run_block(
            carried, query_f, key_f, value_f, logits, log_decay_rate, step_bias, resets
        )

    (local_out, local_end), pull_zero = jax.vjp(from_state, zero_state)
    own_adjoint = pull_zero((cotangent, jnp.zeros_like(local_end)))[0]
    transition = run_block(
        identity, query_f, key_f, jnp.zeros_like(value_f), logits, log_decay_rate, step_bias, resets
    )[1]
    flipped = jnp.swapaxes(transition, 2, 3)
    state_in = entering((transition, local_end), "ctx", compose, (identity, zero_state), False)[1]
    adjoint_out = entering((flipped, own_adjoint), "ctx", compose, (identity, zero_state), True)[1]

    def whole_block(carried, queries_in, keys_in, values_in, logit_rows, rate_logs, biases):
        return run_block(
            carried, queries_in, keys_in, values_in, logit_rows, rate_logs, biases, resets
        )

    primal, pull_all = jax.vjp(
        whole_block, state_in, query_f, key_f, value_f, logits, log_decay_rate, step_bias
    )
    gradients = pull_all((cotangent, adjoint_out))
    logit_grad = gradients[4][0]
    hidden_part = jnp.dot(logit_grad, both_weights.astype(jnp.float32).T, precision=highest)
    hidden_grad = lax.psum_scatter(hidden_part, "dp", scatter_dimension=1, tiled=True).astype(
        jnp.bfloat16
    )
    weight_grad = jnp.dot(hidden_in.astype(jnp.float32).T, logit_grad, precision=highest)
    totals = lax.psum((weight_grad, gradients[5], gradients[6]), "ctx")
    return (
        gradients[1][0].astype(jnp.bfloat16),
        gradients[2][0].astype(jnp.bfloat16),
        gradients[3][0].astype(jnp.bfloat16),
        hidden_grad,
        totals[0][:, :head_count],
        totals[0][:, head_count:],
        totals[1],
        totals[2],
    )


def solution(mesh):
    in_specs = (
        P("ctx", None),
        P("ctx", "dp"),
        P("ctx", "dp"),
        P("ctx", "dp"),
        P("ctx", "dp"),
        P(None, "dp"),
        P(None, "dp"),
        P("dp"),
        P("dp"),
        P(),
    )
    out_specs = (
        P("ctx", "dp"),
        P("ctx", "dp"),
        P("ctx", "dp"),
        P("ctx", "dp"),
        P(None, "dp"),
        P(None, "dp"),
        P("dp"),
        P("dp"),
    )
    return jax.shard_map(
        on_device, mesh=mesh, in_specs=in_specs, out_specs=out_specs, check_vma=False
    )
```

profile of v0, /device:TPU:0, one launch (start us, length us, event | category | flops | bytes accessed | tf_op | source)
XLA Modules:
  0.0 834.3 jit_solution(11889716074259748909)
XLA Ops:
  15.2 88.8 %while.109 = (s32[]{:T(128)}, f32[1,8,128,128]{3,2,1,0:T(8,128)S(1)}, f32[2,1,64]{2,1,0:T(1,128)S(1)}, f32[2,1,8,64]{3,2,1,0:T(8,128)S(1)}, f32[2,1,8,64,128]{4,...) while((s32[]{:T(128)}, ...), condition=%wide.region_15.18_spmd.clone, body=%wide.region_12.17_spmd.clone.sunk | while | flops 303142976 | bytes 4117760 | solution.py:100
  16.5 39.3 %custom-call.41 = f32[1,8,1,64,64]{3,4,2,1,0:T(8,128)S(1)} custom-call(f32[1,8,1,64,64]{4,3,2,1,0:T(8,128)S(1)} %fusion.519), custom_call_target="InvertDiagBlocksLowerTriangular" | custom-call | tf_op jit(solution)/shard_map/jvp()/while/body/eval_jaxpr/triangular_solve/custom-call.1 | solution.py:53
  60.8 39.3 %custom-call.41 = f32[1,8,1,64,64]{3,4,2,1,0:T(8,128)S(1)} custom-call(f32[1,8,1,64,64]{4,3,2,1,0:T(8,128)S(1)} %fusion.519), custom_call_target="InvertDiagBlocksLowerTriangular" | custom-call | tf_op jit(solution)/shard_map/jvp()/while/body/eval_jaxpr/triangular_solve/custom-call.1 | solution.py:53
  104.9 87.2 %while.103 = (s32[]{:T(128)}, f32[1,8,128,128]{3,2,1,0:T(8,128)S(1)}, f32[2,1,64]{2,1,0:T(1,128)S(1)}, f32[2,1,8,64]{3,2,1,0:T(8,128)S(1)}, f32[2,1,8,64,128]{4,...) while((s32[]{:T(128)}, f32[1,8,128,128]{3,2,1,0:T(8,128)S(1)}, ...), condition=%wide.region_4.6_spmd, body=%wide.region_1.5_spmd.sunk | while | flops 302884928 | bytes 3858657 | solution.py:100
  106.3 39.3 %custom-call.36 = f32[1,8,1,64,64]{3,4,2,1,0:T(8,128)S(1)} custom-call(f32[1,8,1,64,64]{4,3,2,1,0:T(8,128)S(1)} %fusion.414), custom_call_target="InvertDiagBlocksLowerTriangular" | custom-call | tf_op jit(solution)/shard_map/while/body/eval_jaxpr/checkpoint/triangular_solve/custom-call.1 | solution.py:53
  149.9 39.3 %custom-call.36 = f32[1,8,1,64,64]{3,4,2,1,0:T(8,128)S(1)} custom-call(f32[1,8,1,64,64]{4,3,2,1,0:T(8,128)S(1)} %fusion.414), custom_call_target="InvertDiagBlocksLowerTriangular" | custom-call | tf_op jit(solution)/shard_map/while/body/eval_jaxpr/checkpoint/triangular_solve/custom-call.1 | solution.py:53
  195.7 99.2 %while.108 = (s32[]{:T(128)}, f32[1,8,128,128]{2,3,1,0:T(8,128)S(1)}, f32[2,1,8,64,128]{4,3,2,1,0:T(8,128)}, f32[2,1,8,64,128]{4,3,2,1,0:T(8,128)S(1)}, f32[2,1,...) while((s32[]{:T(128)}, ...), condition=%wide.region_9.12_spmd.clone, body=%wide.region_6.11_spmd.clone.sunk | while | flops 504735808 | bytes 9574183 | solution.py:100
  199.1 40.0 %custom-call.40 = f32[1,8,1,64,64]{3,4,2,1,0:T(8,128)} custom-call(f32[1,8,1,64,64]{4,3,2,1,0:T(8,128)S(1)} %fusion.507), custom_call_target="InvertDiagBlocksLowerTriangular" | custom-call | tf_op jit(solution)/shard_map/transpose(jvp())/while/body/eval_jaxpr/checkpoint/triangular_solve/custom-call.0 | solution.py:53
  248.7 40.0 %custom-call.40 = f32[1,8,1,64,64]{3,4,2,1,0:T(8,128)} custom-call(f32[1,8,1,64,64]{4,3,2,1,0:T(8,128)S(1)} %fusion.507), custom_call_target="InvertDiagBlocksLowerTriangular" | custom-call | tf_op jit(solution)/shard_map/transpose(jvp())/while/body/eval_jaxpr/checkpoint/triangular_solve/custom-call.0 | solution.py:53
  297.2 90.6 %while.107 = (s32[]{:T(128)}, f32[1,8,128,128]{3,2,1,0:T(8,128)S(1)}, f32[2,1,8,128,128]{4,3,2,1,0:T(8,128)}, f32[2,1,64]{2,1,0:T(1,128)S(1)}, f32[2,1,8,64]{3,2...) while((s32[]{:T(128)}, ...), condition=%wide.region_21.24_spmd.clone, body=%wide.region_18.23_spmd.clone.sunk | while | flops 302880832 | bytes 5166837 | solution.py:100
  298.5 39.3 %custom-call.39 = f32[1,8,1,64,64]{3,4,2,1,0:T(8,128)S(1)} custom-call(f32[1,8,1,64,64]{4,3,2,1,0:T(8,128)S(1)} %fusion.486), custom_call_target="InvertDiagBlocksLowerTriangular" | custom-call | tf_op jit(solution)/shard_map/jvp()/while/body/eval_jaxpr/triangular_solve/custom-call.1 | solution.py:53
  343.8 39.3 %custom-call.39 = f32[1,8,1,64,64]{3,4,2,1,0:T(8,128)S(1)} custom-call(f32[1,8,1,64,64]{4,3,2,1,0:T(8,128)S(1)} %fusion.486), custom_call_target="InvertDiagBlocksLowerTriangular" | custom-call | tf_op jit(solution)/shard_map/jvp()/while/body/eval_jaxpr/triangular_solve/custom-call.1 | solution.py:53
  387.9 62.4 %all-gather.9.cloned.1.call-done = f32[16,8,128,128]{3,2,1,0:T(8,128)} async-done(((f32[1,8,128,128]{3,2,1,0:T(8,128)}), f32[16,8,128,128]{3,2,1,0:T(8,128)}) %all-gather.9.cloned.1.call-update) | async-done | bytes 8388624 | tf_op jit(solution)/shard_map/all_gather | solution.py:18
  450.4 28.9 %while.104 = (s32[]{:T(128)}, f32[1,8,128,128]{3,2,1,0:T(8,128)S(1)}, s32[]{:T(128)}, f32[16,1,8,128,128]{4,3,2,1,0:T(8,128)}, f32[16,1,8,128,128]{4,3,2,1,0:T(8...) while((s32[]{:T(128)}, f32[1,8,128,128]{3,2,1,0:T(8,128)S(1)}, s32[]{:T(128)}, ...), condition=%wide.region_11.14_spmd, body=%wide.region_10.13_spmd.sunk | while | flops 201457664 | bytes 3146891 | solution.py:27
  482.0 232.7 %while.106 = (s32[]{:T(128)}, f32[1,8,128,128]{2,3,1,0:T(8,128)S(1)}, f32[2,1,8,64,128]{4,3,0,2,1:T(8,128)}, f32[2,1,8,64,128]{4,3,0,2,1:T(8,128)}, bf16[2,1,8,6...) while((s32[]{:T(128)}, ...), condition=%wide.region_34.37_spmd, body=%wide.region_22.36_spmd.sunk | while | flops 1389044736 | bytes 36235220 | solution.py:100
  494.9 2.0 constant_dynamic-slice_fusion.7
  500.9 40.7 %custom-call.38 = f32[1,8,1,64,64]{3,4,2,1,0:T(8,128)} custom-call(f32[1,8,1,64,64]{4,3,2,1,0:T(8,128)} %add_bitcast_fusion.2), custom_call_target="InvertDiagBlocksLowerTriangular" | custom-call | tf_op jit(solution)/shard_map/transpose(jvp())/while/body/eval_jaxpr/checkpoint/triangular_solve | solution.py:53
  542.7 40.7 %custom-call.37 = f32[1,8,1,64,64]{3,4,2,1,0:T(8,128)} custom-call(f32[1,8,1,64,64]{4,3,2,1,0:T(8,128)} %get-tuple-element.1956), custom_call_target="InvertDiagBlocksLowerTriangular" | custom-call | tf_op jit(solution)/shard_map/transpose(jvp())/while/body/eval_jaxpr/checkpoint/triangular_solve/custom-call.0 | solution.py:53
  611.8 40.7 %custom-call.38 = f32[1,8,1,64,64]{3,4,2,1,0:T(8,128)} custom-call(f32[1,8,1,64,64]{4,3,2,1,0:T(8,128)} %add_bitcast_fusion.2), custom_call_target="InvertDiagBlocksLowerTriangular" | custom-call | tf_op jit(solution)/shard_map/transpose(jvp())/while/body/eval_jaxpr/checkpoint/triangular_solve | solution.py:53
  653.5 40.7 %custom-call.37 = f32[1,8,1,64,64]{3,4,2,1,0:T(8,128)} custom-call(f32[1,8,1,64,64]{4,3,2,1,0:T(8,128)} %get-tuple-element.1956), custom_call_target="InvertDiagBlocksLowerTriangular" | custom-call | tf_op jit(solution)/shard_map/transpose(jvp())/while/body/eval_jaxpr/checkpoint/triangular_solve/custom-call.0 | solution.py:53
  716.9 2.4 fusion.251
  722.2 30.0 %all-reduce.4 = (f32[8]{0:T(128)}, f32[8]{0:T(128)}) all-reduce(f32[8]{0:T(128)S(1)} %negate_multiply_fusion, f32[8]{0:T(128)S(1)} %get-tuple-element.1506), channel_id=1, replica_groups=mesh['ctx'=16,'dp'=2] {'ctx'}, use_global_device_ids=true, to_apply=%region_42.45 | all-reduce | flops 16 | bytes 128 | tf_op jit(solution)/shard_map/psum | solution.py:169
  759.4 41.9 %all-reduce.7.cloned.1.call-done = f32[2048,16]{0,1:T(8,128)} async-done(((f32[2048,16]{0,1:T(8,128)}), f32[2048,16]{0,1:T(8,128)}) %all-reduce.7.cloned.1.call-update) | async-done | bytes 131088 | tf_op jit(solution)/shard_map/psum | solution.py:169
  802.9 22.6 %reduce-scatter.2.cloned.1.call-done = f32[128,1024]{1,0:T(8,128)} async-done(((f32[128,2048]{1,0:T(8,128)}), f32[128,1024]{1,0:T(8,128)}) %reduce-scatter.2.cloned.1.call-update) | async-done | bytes 524304 | tf_op jit(solution)/shard_map/reduce_scatter | solution.py:165
  (467 shorter events, 165.8 us)
Async XLA Ops:
  7.2 289.9 %all-gather.15.cloned.1.call-start = ((), (), s32[]{:S(2)}) async-start(), calls=%async_computation.6 | async-start | bytes 8912896 | tf_op jit(solution)/shard_map/all_gather | solution.py:18
  8.7 3.0 copy-start.21
  11.8 3.4 copy-start.18
  104.8 192.4 %all-gather.13.cloned.1.call-start = ((), (), s32[]{:S(2)}) async-start(), calls=%async_computation.5 | async-start | bytes 8912896 | tf_op jit(solution)/shard_map/all_gather | solution.py:18
  104.9 88.4 %copy-start.17 = (bf16[128,512]{1,0:T(8,128)(2,1)S(1)}, bf16[128,512]{1,0:T(8,128)(2,1)}, u32[]{:S(2)}) copy-start(bf16[128,512]{1,0:T(8,128)(2,1)} %param.29) | copy-start | bytes 393220
  104.9 89.7 %copy-start.16 = (bf16[128,1024]{1,0:T(8,128)(2,1)S(1)}, bf16[128,1024]{1,0:T(8,128)(2,1)}, u32[]{:S(2)}) copy-start(bf16[128,1024]{1,0:T(8,128)(2,1)} %param.32) | copy-start | bytes 786436
  192.9 195.0 %all-gather.11.cloned.1.call-start = ((), (), s32[]{:S(2)}) async-start(), calls=%async_computation.4 | async-start | bytes 8912896 | tf_op jit(solution)/shard_map/all_gather | solution.py:18
  193.4 2.3 copy-start.12
  195.7 100.3 %copy-start.2 = (f32[1,8,128,128]{3,2,1,0:T(8,128)S(1)}, f32[1,8,128,128]{3,2,1,0:T(8,128)}, u32[]{:S(2)}) copy-start(f32[1,8,128,128]{3,2,1,0:T(8,128)} %copy-done.1) | copy-start | bytes 1572868
  296.0 154.4 %all-gather.9.cloned.1.call-start = ((), (), s32[]{:S(2)}) async-start(), calls=%async_computation.3 | async-start | bytes 8912896 | tf_op jit(solution)/shard_map/all_gather | solution.py:18
  297.0 504.3 %all-reduce.7.cloned.1.call-start = ((), (), s32[]{:S(2)}) async-start(), calls=%async_computation.2 | async-start | bytes 262144 | tf_op jit(solution)/shard_map/psum | solution.py:169
  387.9 91.6 %copy-start.22 = (f32[2,1,64]{2,1,0:T(1,128)}, f32[2,1,64]{2,1,0:T(1,128)S(1)}, u32[]{:S(2)}) copy-start(f32[2,1,64]{2,1,0:T(1,128)S(1)} %get-tuple-element.2293) | copy-start | bytes 1540
  494.9 96.7 %copy-start.4 = (f32[1,8,64,128]{3,2,1,0:T(8,128)}, f32[1,8,64,128]{3,2,1,0:T(8,128)S(1)}, u32[]{:S(2)}) copy-start(f32[1,8,64,128]{3,2,1,0:T(8,128)S(1)} %get-tuple-element.1943) | copy-start | bytes 786436 | tf_op jit(solution)/shard_map/transpose(jvp())/while
  583.4 13.2 %copy-start.9 = (f32[2,1,8,64,128]{4,3,0,2,1:T(8,128)S(1)}, f32[2,1,8,64,128]{4,3,0,2,1:T(8,128)}, u32[]{:S(2)}) copy-start(f32[2,1,8,64,128]{4,3,0,2,1:T(8,128)} %get-tuple-element.2220) | copy-start | bytes 1572868 | tf_op jit(solution)/shard_map/transpose(jvp())/while
  583.4 14.5 %copy-start.7 = (f32[2,1,8,64,128]{4,3,0,2,1:T(8,128)S(1)}, f32[2,1,8,64,128]{4,3,0,2,1:T(8,128)}, u32[]{:S(2)}) copy-start(f32[2,1,8,64,128]{4,3,0,2,1:T(8,128)} %get-tuple-element.2219) | copy-start | bytes 1572868 | tf_op jit(solution)/shard_map/transpose(jvp())/while
  597.2 2.6 copy-start.10
  605.8 96.6 %copy-start.4 = (f32[1,8,64,128]{3,2,1,0:T(8,128)}, f32[1,8,64,128]{3,2,1,0:T(8,128)S(1)}, u32[]{:S(2)}) copy-start(f32[1,8,64,128]{3,2,1,0:T(8,128)S(1)} %get-tuple-element.1943) | copy-start | bytes 786436 | tf_op jit(solution)/shard_map/transpose(jvp())/while
  694.2 13.2 %copy-start.9 = (f32[2,1,8,64,128]{4,3,0,2,1:T(8,128)S(1)}, f32[2,1,8,64,128]{4,3,0,2,1:T(8,128)}, u32[]{:S(2)}) copy-start(f32[2,1,8,64,128]{4,3,0,2,1:T(8,128)} %get-tuple-element.2220) | copy-start | bytes 1572868 | tf_op jit(solution)/shard_map/transpose(jvp())/while
  694.2 14.5 %copy-start.7 = (f32[2,1,8,64,128]{4,3,0,2,1:T(8,128)S(1)}, f32[2,1,8,64,128]{4,3,0,2,1:T(8,128)}, u32[]{:S(2)}) copy-start(f32[2,1,8,64,128]{4,3,0,2,1:T(8,128)} %get-tuple-element.2219) | copy-start | bytes 1572868 | tf_op jit(solution)/shard_map/transpose(jvp())/while
  708.1 2.6 copy-start.10
  714.7 42.6 %copy-start.20 = (f32[128,4]{0,1:T(4,128)S(1)}, f32[128,4]{0,1:T(4,128)}, u32[]{:S(2)}) copy-start(f32[128,4]{0,1:T(4,128)} %copy-done.19) | copy-start | bytes 6148
  714.7 42.9 %copy-start.13 = (bf16[128,512]{0,1:T(8,128)(2,1)S(1)}, bf16[128,512]{0,1:T(8,128)(2,1)}, u32[]{:S(2)}) copy-start(bf16[128,512]{0,1:T(8,128)(2,1)} %copy-done.12) | copy-start | bytes 393220
  714.8 43.8 %copy-start.14 = (bf16[2,1,8,64,128]{4,3,2,1,0:T(8,128)(2,1)S(1)}, bf16[2,1,8,64,128]{4,3,2,1,0:T(8,128)(2,1)}, u32[]{:S(2)}) copy-start(bf16[2,1,8,64,128]{4,3,2,1,0:T(8,128)(2,1)} %get-tuple-element.909) | copy-start | bytes 786436
  716.9 108.6 %reduce-scatter.2.cloned.1.call-start = ((), (), s32[]{:S(2)}) async-start(), calls=%async_computation.1 | async-start | bytes 1572864 | tf_op jit(solution)/shard_map/reduce_scatter | solution.py:165
  (10 other events, 13.7 us)
Sparse Core Ops, SparseCore 0:
  104.9 78.3 all-gather.14
  193.0 78.0 all-gather.12
  296.1 78.3 all-gather.10
  376.5 73.7 all-gather.8
  717.0 84.2 all-reduce.6
  803.4 21.9 reduce-scatter.1
where the time goes:
time: 838 us; the launch traced here: 834 us
  other arithmetic  504 us (60%)
  waiting for transfers between devices  127 us (15%)
  matrix products  102 us (12%)
  local copies, waits for them, and re-layouts  41.9 us (5%)
  blocking collectives  30 us (4%)
  between operations  15.5 us (2%)
  loops' own time  13.1 us (2%)
    another operation x42, other arithmetic, block_step(): lax.linalg.triangular_solve(system, target, left_side=True, lower=True, u...  483 us
    all_gather x4, waiting for transfers between devices, entering(): gathered = jax.tree.map(lambda a: lax.all_gather(a, axis), part)  62.5 us
    psum x1, waiting for transfers between devices, on_device(): totals = lax.psum((weight_grad, gradients[5], gradients[6]), 'ctx')  41.9 us
    psum x1, blocking collectives, on_device(): totals = lax.psum((weight_grad, gradients[5], gradients[6]), 'ctx')  30 us
    dot_general x15, matrix products, apply_map(): jnp.einsum('bhij,bhjk->bhik', matrices, incoming, precision=lax.Precision...  27.8 us
    reduce_scatter x1, waiting for transfers between devices, on_device(): lax.psum_scatter(hidden_part, 'dp', scatter_dimension=1, tiled=True)  22.6 us
  transfers between devices with their start and end apart: 6, of which 3 were waited for; matrix products, arithmetic and copies ran while one was open for 35% of the time, Pallas kernels for 0%

commit v1 on v0

v1 whole, which is shorter than its diff:
```python
import functools

import jax
import jax.numpy as jnp
from jax import lax
from jax.experimental import pallas as pl
from jax.experimental.pallas import tpu as pltpu
from jax.sharding import PartitionSpec as P

DK = 128
DV = 128
LANES = 128
norm_epsilon = 1e-06

MESH = pl.DeviceIdType.MESH
NN = ((1,), (0,))
NT = ((1,), (1,))
TN = ((0,), (0,))
f32 = jnp.float32
bf16 = jnp.bfloat16
VMEM_LIMIT = 56 * 1024 * 1024


def one_pass(a, b, dims):
    return lax.dot_general(a, b, (dims, ((), ())), preferred_element_type=f32)


def split(x):
    if isinstance(x, tuple):
        return x
    if x.dtype == bf16:
        return (x,)
    high = x.astype(bf16)
    return (high, (x - high.astype(f32)).astype(bf16))


def split3(x):
    high = x.astype(bf16)
    rest = x - high.astype(f32)
    middle = rest.astype(bf16)
    return (high, middle, (rest - middle.astype(f32)).astype(bf16))


def mm(a, b, dims=NN):
    a, b = split(a), split(b)
    total = None
    for i, left in enumerate(a):
        for j, right in enumerate(b):
            if i + j < max(len(a), len(b)):
                term = one_pass(left, right, dims)
                total = term if total is None else total + term
    return total


def iotas():
    rows = lax.broadcasted_iota(jnp.int32, (LANES, LANES), 0)
    columns = lax.broadcasted_iota(jnp.int32, (LANES, LANES), 1)
    return rows, columns


def as_row(eye, column):
    return jnp.sum(jnp.where(eye, column, 0.0), axis=0, keepdims=True)


def as_column(eye, row):
    return jnp.sum(jnp.where(eye, row, 0.0), axis=1, keepdims=True)


def rsum(x):
    return jnp.sum(x, axis=1, keepdims=True)


def gates(logits, rate_row, bias_row, heads):
    x = logits + bias_row
    softplus = jnp.maximum(x, 0.0) + jnp.log1p(jnp.exp(-jnp.abs(x)))
    return -jnp.exp(rate_row) * softplus


def sigmoid(x):
    return 1.0 / (1.0 + jnp.exp(-x))


def scales(raw):
    wide = raw.astype(f32)
    return lax.rsqrt(rsum(wide * wide) + norm_epsilon)


def head_slice(ref, index):
    return ref[:, index * 128 : (index + 1) * 128]


def segment(doc, offset, size):
    inside = jnp.logical_and(doc >= offset, doc < offset + size)
    place = jnp.where(inside, doc - offset, size)
    return place


def decay_parts(eye, lower, rows, columns, cum_col, place):
    cum_row = as_row(eye, cum_col)
    keep = jnp.logical_and(lower, (rows >= place) == (columns >= place))
    decay = jnp.where(keep, jnp.exp(jnp.where(keep, cum_col - cum_row, 0.0)), 0.0)
    places = rows[:, :1]
    carry = jnp.where(places < place, jnp.exp(cum_col), 0.0)
    last = cum_col[LANES - 1 : LANES, :]
    same = jnp.logical_or(places >= place, place >= LANES)
    to_last = jnp.where(same, jnp.exp(jnp.where(same, last - cum_col, 0.0)), 0.0)
    return decay, carry, to_last, carry[LANES - 1 : LANES, :]


def first_kernel(
    heads, place_ref, hid_ref, w_ref, q_ref, k_ref, v_ref, do_ref, rate_ref, bias_ref,
    a_ref, b_ref, n_ref, t_ref, w_out_ref, u_ref, p_ref, logit_ref, cum_ref,
):
    rows, columns = iotas()
    eye = rows == columns
    lower = rows >= columns
    strict = rows > columns
    place = place_ref[0]
    logits = one_pass(hid_ref[...], w_ref[...], NN)
    logit_ref[...] = logits
    log_decay = gates(logits, rate_ref[...], bias_ref[...], heads)
    ones = lower.astype(f32).astype(bf16)
    cum = mm(ones, split3(log_decay))
    cum_ref[...] = cum
    beta_all = sigmoid(logits)
    eye_f = eye.astype(f32)
    group = heads // (q_ref.shape[1] // DK)
    decays, betas, rks, rqs, couplings = [], [], [], [], []
    for h in range(heads):
        if h % group == 0:
            kb, qb = head_slice(k_ref, h // group), head_slice(q_ref, h // group)
            rk = scales(kb)
            rq = scales(qb) * DK ** (-0.5)
            rk_row = as_row(eye, rk)
            gram = one_pass(kb, kb, NT) * rk * rk_row
            query_key = one_pass(qb, kb, NT) * rq * rk_row
        parts = decay_parts(eye, lower, rows, columns, cum[:, h : h + 1], place)
        beta = beta_all[:, heads + h : heads + h + 1]
        couplings.append(jnp.where(strict, beta * parts[0] * gram, 0.0))
        p_ref[h] = query_key * parts[0]
        decays.append(parts[1:])
        betas.append(beta)
        rks.append(rk)
        rqs.append(rq)
    inverses = []
    pair = jnp.logical_and(strict, rows // 2 == columns // 2)
    for h in range(heads):
        inverses.append(eye_f - jnp.where(pair, couplings[h], 0.0))
    size = 2
    while size < LANES:
        band = jnp.logical_and(
            rows // (2 * size) == columns // (2 * size), rows // size > columns // size
        )
        held = [split(x) for x in inverses]
        middles = [
            mm(split(jnp.where(band, couplings[h], 0.0)), held[h]) for h in range(heads)
        ]
        inverses = [inverses[h] - mm(held[h], middles[h]) for h in range(heads)]
        size *= 2
    for h in range(heads):
        kb, qb = head_slice(k_ref, h // group), head_slice(q_ref, h // group)
        vb, dob = head_slice(v_ref, h), head_slice(do_ref, h)
        carry, to_last, last_carry = decays[h]
        beta, rk, rq = betas[h], rks[h], rqs[h]
        inverse = inverses[h]
        t_ref[h] = inverse
        w = mm(inverse * as_row(eye, beta * carry * rk), kb)
        u = mm(inverse * as_row(eye, beta), vb)
        w_out_ref[h] = w
        u_ref[h] = u
        weight = rk * to_last
        a_ref[h] = last_carry * eye_f - mm(kb, w * weight, TN)
        b_ref[h] = mm(kb, u * weight, TN)
        reach = (carry * rq) * qb.astype(f32) - mm(p_ref[h], w)
        n_ref[h] = mm(reach, dob, TN)


def chain_kernel(
    count, names, half, a_ref, b_ref, n_ref, s_ref, l_ref,
    pa, pb, pn, s_in, l_in, s_send, l_send, s_give, l_give, ca, cb, cn,
    swap_send, swap_recv, s_ss, s_rs, l_ss, l_rs, g_send, g_recv,
):
    ctx, dp = names
    me = lax.axis_index(ctx)
    core = lax.rem(me, 2)
    chip = me // 2
    chips = count // 2
    mate = me + 1 - 2 * core

    def at(place):
        return {ctx: place}

    barrier = pltpu.get_barrier_semaphore()
    pl.semaphore_signal(barrier, inc=1, device_id=at(mate), device_id_type=MESH)

    @pl.when(chip > 0)
    def _():
        pl.semaphore_signal(barrier, inc=1, device_id=at(me - 2), device_id_type=MESH)

    @pl.when(chip < chips - 1)
    def _():
        pl.semaphore_signal(barrier, inc=1, device_id=at(me + 2), device_id_type=MESH)

    around = 1 + (chip > 0).astype(jnp.int32) + (chip < chips - 1).astype(jnp.int32)
    pl.semaphore_wait(barrier, around)

    mine = core * half
    theirs = (1 - core) * half
    swaps = []
    for i, (source, target) in enumerate(((a_ref, pa), (b_ref, pb), (n_ref, pn))):
        copy = pltpu.make_async_remote_copy(
            src_ref=source.at[pl.ds(theirs, half)], dst_ref=target,
            send_sem=swap_send.at[i], recv_sem=swap_recv.at[i],
            device_id=at(mate), device_id_type=MESH,
        )
        copy.start()
        swaps.append(copy)
    for copy in swaps:
        copy.wait()

    def compose(first_a, first_b, first_n, second_a, second_b, second_n):
        for h in range(half):
            later = split(second_a(h))
            earlier = split(first_a(h))
            ca[h] = mm(later, earlier)
            cb[h] = mm(later, first_b(h)) + second_b(h)
            cn[h] = mm(earlier, second_n(h), TN) + first_n(h)

    own = [lambda h, r=r: r[mine + h] for r in (a_ref, b_ref, n_ref)]
    other = [lambda h, r=r: r[h] for r in (pa, pb, pn)]

    @pl.when(core == 0)
    def _():
        compose(*own, *other)

    @pl.when(core == 1)
    def _():
        compose(*other, *own)

    def s_copy(h):
        return pltpu.make_async_remote_copy(
            src_ref=s_send.at[h], dst_ref=s_in.at[h], send_sem=s_ss.at[h],
            recv_sem=s_rs.at[h], device_id=at(me + 2), device_id_type=MESH,
        )

    def l_copy(h):
        return pltpu.make_async_remote_copy(
            src_ref=l_send.at[h], dst_ref=l_in.at[h], send_sem=l_ss.at[h],
            recv_sem=l_rs.at[h], device_id=at(me - 2), device_id_type=MESH,
        )

    def forward():
        for h in range(half):

            @pl.when(chip == 0)
            def _():
                s_in[h] = jnp.zeros((DK, DV), f32)
                s_send[h] = cb[h]

            @pl.when(chip > 0)
            def _():
                s_copy(h).wait_recv()

                @pl.when(chip < chips - 1)
                def _():
                    s_send[h] = mm(ca[h], s_in[h]) + cb[h]

            @pl.when(chip < chips - 1)
            def _():
                s_copy(h).start()

    def backward():
        for h in range(half):

            @pl.when(chip == chips - 1)
            def _():
                l_in[h] = jnp.zeros((DK, DV), f32)
                l_send[h] = cn[h]

            @pl.when(chip < chips - 1)
            def _():
                l_copy(h).wait_recv()

                @pl.when(chip > 0)
                def _():
                    l_send[h] = mm(ca[h], l_in[h], TN) + cn[h]

            @pl.when(chip > 0)
            def _():
                l_copy(h).start()

    def give(source, target, i):
        return pltpu.make_async_remote_copy(
            src_ref=source, dst_ref=target.at[pl.ds(mine, half)], send_sem=g_send.at[i],
            recv_sem=g_recv.at[i], device_id=at(mate), device_id_type=MESH,
        )

    def finish_s():
        @pl.when(core == 0)
        def _():
            for h in range(half):
                s_ref[mine + h] = s_in[h]
                s_give[h] = mm(a_ref[mine + h], s_in[h]) + b_ref[mine + h]

        @pl.when(core == 1)
        def _():
            for h in range(half):
                s_ref[mine + h] = mm(pa[h], s_in[h]) + pb[h]
                s_give[h] = s_in[h]

        give(s_give, s_ref, 0).start()

    def finish_l():
        @pl.when(core == 1)
        def _():
            for h in range(half):
                l_ref[mine + h] = l_in[h]
                l_give[h] = mm(a_ref[mine + h], l_in[h], TN) + n_ref[mine + h]

        @pl.when(core == 0)
        def _():
            for h in range(half):
                l_ref[mine + h] = mm(pa[h], l_in[h], TN) + pn[h]
                l_give[h] = l_in[h]

        give(l_give, l_ref, 1).start()

    @pl.when(2 * chip < chips)
    def _():
        forward()
        finish_s()
        backward()
        finish_l()

    @pl.when(2 * chip >= chips)
    def _():
        backward()
        finish_l()
        forward()
        finish_s()

    for h in range(half):

        @pl.when(chip < chips - 1)
        def _():
            s_copy(h).wait_send()

        @pl.when(chip > 0)
        def _():
            l_copy(h).wait_send()

    for i, (source, target) in enumerate(((s_give, s_ref), (l_give, l_ref))):
        give(source, target, i).wait_send()
        give(source, target, i).wait_recv()


def last_kernel(
    heads, place_ref, hid_ref, q_ref, k_ref, v_ref, do_ref, rate_ref, bias_ref,
    t_ref, w_ref, u0_ref, p_ref, logit_ref, cum_ref, s_ref, l_ref,
    dq_ref, dk_ref, dv_ref, lg_ref, wg_ref, small_ref,
):
    rows, columns = iotas()
    eye = rows == columns
    lower = rows >= columns
    strict = rows > columns
    place = place_ref[0]
    logits = logit_ref[...]
    cum = cum_ref[...]
    beta_all = sigmoid(logits)
    last_row = rows[:, :1] == LANES - 1
    group = heads // (q_ref.shape[1] // DK)
    cum_grad = jnp.zeros((LANES, LANES), f32)
    beta_grad = jnp.zeros((LANES, LANES), f32)
    for h in range(heads):
        if h % group == 0:
            kb, qb = head_slice(k_ref, h // group), head_slice(q_ref, h // group)
            kf, qf = kb.astype(f32), qb.astype(f32)
            rk = scales(kb)
            rq0 = scales(qb)
            rq = rq0 * DK ** (-0.5)
            rk_row = as_row(eye, rk)
            gram = one_pass(kb, kb, NT) * rk * rk_row
            query_key = one_pass(qb, kb, NT) * rq * rk_row
            score_sum = jnp.zeros((LANES, LANES), f32)
            gram_sum = jnp.zeros((LANES, LANES), f32)
            q_hat_grad = jnp.zeros((LANES, DK), f32)
            k_hat_grad = jnp.zeros((LANES, DK), f32)
        vb, dob = head_slice(v_ref, h), head_slice(do_ref, h)
        dof = dob.astype(f32)
        decay, carry, to_last, last_carry = decay_parts(
            eye, lower, rows, columns, cum[:, h : h + 1], place
        )
        beta = beta_all[:, heads + h : heads + h + 1]
        state_f, adjoint_f = s_ref[h], l_ref[h]
        state, adjoint = split(state_f), split(adjoint_f)
        key_state = mm(kb, state) * rk
        query_state = mm(qb, state) * rq
        updates_f = u0_ref[h] - mm(w_ref[h], state)
        updates = split(updates_f)
        update_grad = mm(p_ref[h], dob, TN) + mm(kb, adjoint) * (rk * to_last)
        score_grad = mm(dob, updates, NT) * decay
        z_f = mm(t_ref[h], update_grad, TN)
        z = split(z_f)
        dv_ref[:, h * DV : (h + 1) * DV] = (beta * z_f).astype(bf16)
        coupling_grad = jnp.where(strict, -mm(z, updates, NT), 0.0) * decay
        gram_grad = coupling_grad * beta
        last_keys = mm(updates, adjoint, NT)
        q_hat_grad += carry * mm(dob, state, NT)
        k_hat_grad += last_keys * to_last - (beta * carry) * mm(z, state, NT)
        score_sum += score_grad
        gram_sum += gram_grad
        value_f = vb.astype(f32)
        along = coupling_grad * gram
        beta_col = rsum(z_f * (value_f - carry * key_state)) + rsum(along)
        carry_grad = rsum(dof * query_state) - beta * rsum(z_f * key_state)
        spread = score_grad * query_key + along * beta
        to_last_grad = rsum(last_keys * kf) * rk * to_last
        whole = jnp.sum(adjoint_f * state_f, keepdims=True) * last_carry
        whole = whole + jnp.sum(to_last_grad, axis=0, keepdims=True)
        cum_col = (
            rsum(spread)
            - as_column(eye, jnp.sum(spread, axis=0, keepdims=True))
            - to_last_grad
            + carry_grad * carry
            + jnp.where(last_row, whole, 0.0)
        )
        cum_grad = jnp.where(columns == h, cum_col, cum_grad)
        beta_grad = jnp.where(columns == heads + h, beta_col, beta_grad)
        if h % group == group - 1:
            q_hat_grad += mm(score_sum * rk_row, kb)
            k_hat_grad += (
                mm(score_sum * rq, qb, TN)
                + mm(gram_sum * rk_row, kb)
                + mm(gram_sum * rk, kb, TN)
            )
            q_dot = rsum(q_hat_grad * qf)
            k_dot = rsum(k_hat_grad * kf)
            place_q = slice((h // group) * DK, (h // group + 1) * DK)
            dq_ref[:, place_q] = (rq * (q_hat_grad - qf * (rq0 * rq0 * q_dot))).astype(bf16)
            dk_ref[:, place_q] = (rk * (k_hat_grad - kf * (rk * rk * k_dot))).astype(bf16)
    ones = lower.astype(f32).astype(bf16)
    decay_grad = mm(ones, split3(cum_grad), TN)
    log_decay = gates(logits, rate_ref[...], bias_ref[...], heads)
    x = logits + bias_ref[...]
    decay_logit = decay_grad * (-jnp.exp(rate_ref[...])) * sigmoid(x)
    logit_grad = jnp.where(
        columns < heads, decay_logit, beta_grad * beta_all * (1.0 - beta_all)
    )
    logit_grad = jnp.where(columns < 2 * heads, logit_grad, 0.0)
    lg_ref[...] = logit_grad.T[: 2 * heads, :]
    small_ref[0:1, :] = jnp.sum(decay_grad * log_decay, axis=0, keepdims=True)
    small_ref[1:2, :] = jnp.sum(decay_logit, axis=0, keepdims=True)
    wg_ref[...] = mm(split3(logit_grad), hid_ref[...], TN)[: 2 * heads, :]


def sum_kernel(
    sizes, names, x_ref, lg_ref, w_ref, sum_ref, hid_ref,
    parts, total, logits, ss, rs, ss2, rs2, lss, lrs,
):
    count, dp_count = sizes
    ctx, dp = names
    me = lax.axis_index(ctx)
    row = lax.axis_index(dp)

    barrier = pltpu.get_barrier_semaphore()

    def greet(step, _):
        peer = lax.rem(me + step, count)
        pl.semaphore_signal(barrier, inc=1, device_id={ctx: peer}, device_id_type=MESH)
        return 0

    def greet_row(step, _):
        peer = lax.rem(row + step, dp_count)
        pl.semaphore_signal(barrier, inc=1, device_id={dp: peer}, device_id_type=MESH)
        return 0

    lax.fori_loop(1, count, greet, 0)
    lax.fori_loop(1, dp_count, greet_row, 0)
    pl.semaphore_wait(barrier, count - 1 + dp_count - 1)

    def logit_copy(step):
        peer = lax.rem(row + step, dp_count)
        return pltpu.make_async_remote_copy(
            src_ref=lg_ref, dst_ref=logits.at[row], send_sem=lss.at[step],
            recv_sem=lrs.at[step], device_id={dp: peer}, device_id_type=MESH,
        )

    def scatter(step):
        peer = lax.rem(me + step, count)
        return pltpu.make_async_remote_copy(
            src_ref=x_ref.at[peer], dst_ref=parts.at[me], send_sem=ss.at[step],
            recv_sem=rs.at[step], device_id={ctx: peer}, device_id_type=MESH,
        )

    def gather(step):
        peer = lax.rem(me + step, count)
        return pltpu.make_async_remote_copy(
            src_ref=total, dst_ref=sum_ref.at[me], send_sem=ss2.at[step],
            recv_sem=rs2.at[step], device_id={ctx: peer}, device_id_type=MESH,
        )

    def each(last, act):
        def body(step, _):
            act(step)
            return 0

        lax.fori_loop(1, last, body, 0)

    each(count, lambda step: scatter(step).start())
    each(dp_count, lambda step: logit_copy(step).start())
    parts[me] = x_ref[me]
    logits[row] = lg_ref[...]
    each(count, lambda step: scatter(step).wait_recv())
    amount = parts[0]
    for i in range(1, count):
        amount = amount + parts[i]
    total[...] = amount
    sum_ref[me] = amount
    each(count, lambda step: gather(step).start())
    each(dp_count, lambda step: logit_copy(step).wait_recv())
    hidden = None
    for d in range(dp_count):
        term = mm(split3(logits[d]), w_ref[d], TN)
        hidden = term if hidden is None else hidden + term
    hid_ref[...] = hidden.astype(bf16)
    each(count, lambda step: gather(step).wait_recv())
    each(count, lambda step: scatter(step).wait_send())
    each(count, lambda step: gather(step).wait_send())
    each(dp_count, lambda step: logit_copy(step).wait_send())


def on_device(
    sizes, hidden_in, query_vectors, key_vectors, value_vectors, out_cotangent,
    w_decay, w_beta, log_decay_rate, step_bias, doc_start,
):
    count, dp_count = sizes
    tokens, width = hidden_in.shape
    heads = log_decay_rate.shape[0]
    names = ("ctx", "dp")
    vmem = pl.BlockSpec(memory_space=pltpu.VMEM)
    smem = pl.BlockSpec(memory_space=pltpu.SMEM)
    params = functools.partial(pltpu.CompilerParams, vmem_limit_bytes=VMEM_LIMIT)
    both = jnp.concatenate([w_decay, w_beta], axis=1)
    panel_w = jnp.pad(both, ((0, 0), (0, LANES - 2 * heads)))
    rate_row = jnp.pad(log_decay_rate, (0, LANES - heads))[None]
    bias_row = jnp.pad(step_bias, (0, LANES - heads))[None]
    offset = lax.axis_index("ctx") * tokens
    place = segment(doc_start, offset, tokens)
    piece = width // dp_count
    features = lax.all_gather(both.T, "dp")
    features = lax.dynamic_slice_in_dim(
        features, lax.axis_index("dp") * piece, piece, axis=2
    )

    square = jax.ShapeDtypeStruct((heads, LANES, LANES), f32)
    panel = jax.ShapeDtypeStruct((LANES, LANES), f32)
    a, b, n, t, w, u, p, logits, cum = pl.pallas_call(
        functools.partial(first_kernel, heads),
        out_shape=(square,) * 7 + (panel,) * 2,
        in_specs=[smem] + [vmem] * 8,
        out_specs=(vmem,) * 9,
        compiler_params=params(),
        name="local_maps",
    )(
        place, hidden_in, panel_w, query_vectors, key_vectors, value_vectors,
        out_cotangent, rate_row, bias_row,
    )

    half = heads // 2
    held = pltpu.VMEM((half, DK, DV), f32)
    dma = pltpu.SemaphoreType.DMA
    state, adjoint = pl.pallas_call(
        functools.partial(chain_kernel, count, names, half),
        out_shape=(square,) * 2,
        in_specs=[vmem] * 3,
        out_specs=(vmem,) * 2,
        scratch_shapes=[held] * 12
        + [dma((3,)), dma((3,))]
        + [dma((half,))] * 4
        + [dma((2,)), dma((2,))],
        compiler_params=params(collective_id=0, has_side_effects=True),
        name="chain",
    )(a, b, n)

    query_grad, key_grad, value_grad, logit_grad, weight_grad, small = pl.pallas_call(
        functools.partial(last_kernel, heads),
        out_shape=(
            jax.ShapeDtypeStruct(query_vectors.shape, bf16),
            jax.ShapeDtypeStruct(key_vectors.shape, bf16),
            jax.ShapeDtypeStruct(value_vectors.shape, bf16),
            jax.ShapeDtypeStruct((2 * heads, LANES), f32),
            jax.ShapeDtypeStruct((2 * heads, width), f32),
            jax.ShapeDtypeStruct((2, LANES), f32),
        ),
        in_specs=[smem] + [vmem] * 15,
        out_specs=(vmem,) * 6,
        compiler_params=params(),
        name="gradients",
    )(
        place, hidden_in, query_vectors, key_vectors, value_vectors, out_cotangent,
        rate_row, bias_row, t, w, u, p, logits, cum, state, adjoint,
    )

    lines = 2 * heads * width // LANES
    per = -(-lines // count)
    stacked = weight_grad.reshape(lines, LANES)
    stacked = jnp.pad(stacked, ((0, per * count - lines), (0, 0))).reshape(count, per, LANES)
    stacked = jnp.concatenate(
        [stacked, jnp.broadcast_to(small[None], (count, 2, LANES))], axis=1
    )
    summed, hidden_grad = pl.pallas_call(
        functools.partial(sum_kernel, sizes, names),
        out_shape=(
            jax.ShapeDtypeStruct(stacked.shape, f32),
            jax.ShapeDtypeStruct((tokens, piece), bf16),
        ),
        in_specs=[vmem] * 3,
        out_specs=(vmem,) * 2,
        scratch_shapes=[
            pltpu.VMEM(stacked.shape, f32),
            pltpu.VMEM(stacked.shape[1:], f32),
            pltpu.VMEM((dp_count,) + logit_grad.shape, f32),
        ]
        + [dma((count,))] * 4
        + [dma((dp_count,))] * 2,
        compiler_params=params(collective_id=1, has_side_effects=True),
        name="totals",
    )(stacked, logit_grad, features)
    weights = summed[:, :per].reshape(per * count, LANES)[:lines].reshape(2 * heads, width).T
    return (
        query_grad,
        key_grad,
        value_grad,
        hidden_grad,
        weights[:, :heads],
        weights[:, heads:],
        summed[0, per, :heads],
        summed[0, per + 1, :heads],
    )


def solution(mesh):
    in_specs = (
        P("ctx", None),
        P("ctx", "dp"),
        P("ctx", "dp"),
        P("ctx", "dp"),
        P("ctx", "dp"),
        P(None, "dp"),
        P(None, "dp"),
        P("dp"),
        P("dp"),
        P(),
    )
    out_specs = (
        P("ctx", "dp"),
        P("ctx", "dp"),
        P("ctx", "dp"),
        P("ctx", "dp"),
        P(None, "dp"),
        P(None, "dp"),
        P("dp"),
        P("dp"),
    )
    sizes = (mesh.shape["ctx"], mesh.shape["dp"])
    return jax.shard_map(
        functools.partial(on_device, sizes),
        mesh=mesh,
        in_specs=in_specs,
        out_specs=out_specs,
        check_vma=False,
    )
```

time: 838 us -> 97.5 us (0.12)
  other arithmetic: 504 us -> 0.69 us
  waiting for transfers between devices: 127 us -> 0 us
  matrix products: 102 us -> 0 us
  Pallas kernels: 0 us -> 80 us
  local copies, waits for them, and re-layouts: 41.9 us -> 9.15 us
  blocking collectives: 30 us -> 5.85 us
  between operations: 15.5 us -> 1.38 us
  loops' own time: 13.1 us -> 0 us
    another operation x78 -> x0, other arithmetic: 489 us -> none  [the longest x42 483 us: block_step(): lax.linalg.triangular_solve(system, target, left_side=True, lower=True, u...]
    dot_general x82 -> x0, matrix products: 85.7 us -> none  [the longest x15 27.8 us: apply_map(): jnp.einsum('bhij,bhjk->bhik', matrices, incoming, precision=lax.Precision...]
    pallas_call x0 -> x4, Pallas kernels: none -> 80 us  [the longest x1 45.2 us: on_device(): pl.pallas_call(functools.partial(chain_kernel, count, names, half), out_s...]
    all_gather x4 -> x0, waiting for transfers between devices: 62.5 us -> none  [entering(): gathered = jax.tree.map(lambda a: lax.all_gather(a, axis), part)]
    psum x1 -> x0, waiting for transfers between devices: 41.9 us -> none  [on_device(): totals = lax.psum((weight_grad, gradients[5], gradients[6]), 'ctx')]
    psum x1 -> x0, blocking collectives: 30 us -> none  [on_device(): totals = lax.psum((weight_grad, gradients[5], gradients[6]), 'ctx')]
    reduce_scatter x1 -> x0, waiting for transfers between devices: 22.6 us -> none  [on_device(): lax.psum_scatter(hidden_part, 'dp', scatter_dimension=1, tiled=True)]
    another operation x14 -> x0, matrix products: 16.2 us -> none  [block_step(): lax.linalg.triangular_solve(system, target, left_side=True, lower=True, u...]
  transfers between devices with their start and end apart: 6 -> 0, of which waited for: 3 -> 0; matrix products, arithmetic and copies ran while one was open for 35% -> 0% of each run, Pallas kernels for 0% -> 0%
where the time goes in v1:
time: 97.5 us; the launch traced here: 97.1 us
  Pallas kernels  80 us (82%)
  local copies, waits for them, and re-layouts  9.15 us (9%)
  blocking collectives  5.85 us (6%)
  between operations  1.38 us (1%)
    pallas_call x1, Pallas kernels, on_device(): pl.pallas_call(functools.partial(chain_kernel, count, names, half), out_s...  45.2 us
    pallas_call x1, Pallas kernels, on_device(): pl.pallas_call(functools.partial(sum_kernel, sizes, names), out_shape=(ja...  14.9 us
    pallas_call x1, Pallas kernels, on_device(): pl.pallas_call(functools.partial(last_kernel, heads), out_shape=(jax.Shap...  10.1 us
    pallas_call x1, Pallas kernels, on_device(): pl.pallas_call(functools.partial(first_kernel, heads), out_shape=(square,...  9.79 us
    all_gather x1, blocking collectives, on_device(): features = lax.all_gather(both.T, 'dp')  5.85 us
    unnamed x16, local copies, waits for them, and re-layouts  3.95 us

profile of v1, /device:TPU:0, one launch (start us, length us, event | category | flops | bytes accessed | tf_op | source)
XLA Modules:
  0.0 97.1 jit_solution(8028657120747239230)
XLA Ops:
  0.6 0.0 copy-start.1
  1.3 0.0 copy-start.4
  1.3 0.0 copy-start.5
  1.3 0.6 copy-done.4
  2.0 0.0 copy-done.5
  2.0 0.5 pad_bitcast_fusion
  2.5 0.0 copy-done.1
  2.5 0.8 copy-done.2
  3.3 5.9 %all-gather = bf16[32,2048]{1,0:T(8,128)(2,1)S(1)} all-gather(bf16[16,2048]{1,0:T(8,128)(2,1)S(1)} %bitcast.24), channel_id=2, replica_groups=mesh['ctx'=16,'dp'=2] {'dp'}, dimensions={0}, use_global_device_ids=true | all-gather | bytes 196608 | tf_op jit(solution)/shard_map/all_gather | solution.py:550
  9.1 0.6 constant_dynamic-slice_fusion.w_ref
  9.7 0.3 copy.21
  10.0 0.9 pad.13.w_ref
  10.9 9.8 %local_maps.1 = (f32[8,128,128]{2,1,0:T(8,128)}, f32[8,128,128]{2,1,0:T(8,128)}, f32[8,128,128]{2,1,0:T(8,128)}, f32[8,128,128]{2,1,0:T(8,128)}, f32[8,128,128]{...) custom-call(s32[1]{0:T(128)S(6)} %select_n.7.place_ref, ...), custom_call_target="tpu_custom_call" | custom-call | tf_op jit(solution)/shard_map/local_maps/pallas_call | solution.py:557
  20.7 45.2 %chain.1 = (f32[8,128,128]{2,1,0:T(8,128)}, f32[8,128,128]{2,1,0:T(8,128)}) custom-call(f32[8,128,128]{2,1,0:T(8,128)} %get-tuple-element.33.a_ref, f32[8,128,128]{2,1,0:T(8,128)} %get-tuple-element.34.b_ref, f32[8,128,128]{2,1,0:T(8,128)} %get-tuple-element.35.n_ref), custom_call_target="tpu_custom_call" | custom-call | tf_op jit(solution)/shard_map/chain/pallas_call | solution.py:572
  66.0 10.1 %gradients.1 = (bf16[128,512]{1,0:T(8,128)(2,1)}, bf16[128,512]{1,0:T(8,128)(2,1)}, bf16[128,1024]{1,0:T(8,128)(2,1)}, f32[16,128]{1,0:T(8,128)}, f32[16,2048]{1,0:T(8,128)}, /*index=5*/f32[2,128]{1,0:T(2,128)}) custom-call(s32[1]{0:T(128)S(6)} %select_n.7.place_ref, bf16[128,2048]{1,0:T(8,128)(2,1)} %hid_ref.3, bf16[128,512]{1,0:T(8,128)(2,1)} %q_ref.3, ...), custom_call_target="tpu_custom_call" | custom-call | tf_op jit(solution)/shard_map/gradients/pallas_call | solution.py:585
  76.0 0.6 copy-done.3
  76.7 0.9 copy.22
  77.6 0.7 pad_maximum_fusion.x_ref
  78.3 14.9 %totals.1 = (f32[16,18,128]{2,1,0:T(8,128)}, bf16[128,1024]{1,0:T(8,128)(2,1)}) custom-call(f32[16,18,128]{2,1,0:T(8,128)} %pad_maximum_fusion.x_ref, f32[16,128]{1,0:T(8,128)} %get-tuple-element.43.lg_ref, bf16[2,16,1024]{2,1,0:T(8,128)(2,1)} %constant_dynamic-slice_fusion.w_ref), custom_call_target="tpu_custom_call" | custom-call | tf_op jit(solution)/shard_map/totals/pallas_call | solution.py:611
  93.2 1.3 %slice_bitcast_fusion = (f32[8]{0:T(128)}, f32[8]{0:T(128)}) fusion(f32[16,18,128]{2,1,0:T(8,128)} %get-tuple-element.45), kind=kLoop, calls=%fused_computation.4 | loop fusion | bytes 128 | tf_op jit(solution)/shard_map/squeeze | solution.py:638
  94.5 0.9 slice.15
  95.5 0.7 fusion
  96.1 0.2 copy-done
  96.4 0.7 copy.29
  (7 shorter events, 0.1 us)
Async XLA Ops:
  0.6 1.9 %copy-start.1 = (bf16[2048,8]{0,1:T(8,128)(2,1)S(1)}, bf16[2048,8]{0,1:T(8,128)(2,1)}, u32[]{:S(2)}) copy-start(bf16[2048,8]{0,1:T(8,128)(2,1)} %param.15) | copy-start | bytes 98308
  1.3 0.7 copy-start.4
  1.3 0.7 copy-start.5
  2.5 0.8 copy-start.2
  76.0 0.6 copy-start.3
  95.4 1.0 copy-start

commit v2 on v1

--- a/solution.py
+++ b/solution.py
@@ -109,14 +109,16 @@
 
 def first_kernel(
     heads, place_ref, hid_ref, w_ref, q_ref, k_ref, v_ref, do_ref, rate_ref, bias_ref,
-    a_ref, b_ref, n_ref, t_ref, w_out_ref, u_ref, p_ref, logit_ref, cum_ref,
+    wide_ref, a_ref, b_ref, n_ref, t_ref, w_out_ref, u_ref, p_ref, logit_ref, cum_ref,
 ):
     rows, columns = iotas()
     eye = rows == columns
     lower = rows >= columns
     strict = rows > columns
     place = place_ref[0]
-    logits = one_pass(hid_ref[...], w_ref[...], NN)
+    wide_ref[...] = jnp.zeros_like(wide_ref)
+    wide_ref[0 : 2 * heads, :] = w_ref[...]
+    logits = one_pass(hid_ref[...], wide_ref[...].astype(bf16), NT)
     logit_ref[...] = logits
     log_decay = gates(logits, rate_ref[...], bias_ref[...], heads)
     ones = lower.astype(f32).astype(bf16)
@@ -177,7 +179,7 @@
 
 def chain_kernel(
     count, names, half, a_ref, b_ref, n_ref, s_ref, l_ref,
-    pa, pb, pn, s_in, l_in, s_send, l_send, s_give, l_give, ca, cb, cn,
+    pa, pb, pn, s_in, l_in, s_send, l_send, s_give, l_give, ca, ca_low, cb, cn,
     swap_send, swap_recv, s_ss, s_rs, l_ss, l_rs, g_send, g_recv,
 ):
     ctx, dp = names
@@ -190,20 +192,6 @@
     def at(place):
         return {ctx: place}
 
-    barrier = pltpu.get_barrier_semaphore()
-    pl.semaphore_signal(barrier, inc=1, device_id=at(mate), device_id_type=MESH)
-
-    @pl.when(chip > 0)
-    def _():
-        pl.semaphore_signal(barrier, inc=1, device_id=at(me - 2), device_id_type=MESH)
-
-    @pl.when(chip < chips - 1)
-    def _():
-        pl.semaphore_signal(barrier, inc=1, device_id=at(me + 2), device_id_type=MESH)
-
-    around = 1 + (chip > 0).astype(jnp.int32) + (chip < chips - 1).astype(jnp.int32)
-    pl.semaphore_wait(barrier, around)
-
     mine = core * half
     theirs = (1 - core) * half
     swaps = []
@@ -222,7 +210,7 @@
         for h in range(half):
             later = split(second_a(h))
             earlier = split(first_a(h))
-            ca[h] = mm(later, earlier)
+            ca[h], ca_low[h] = split(mm(later, earlier))
             cb[h] = mm(later, first_b(h)) + second_b(h)
             cn[h] = mm(earlier, second_n(h), TN) + first_n(h)
 
@@ -263,7 +251,7 @@
 
                 @pl.when(chip < chips - 1)
                 def _():
-                    s_send[h] = mm(ca[h], s_in[h]) + cb[h]
+                    s_send[h] = mm((ca[h], ca_low[h]), s_in[h]) + cb[h]
 
             @pl.when(chip < chips - 1)
             def _():
@@ -283,7 +271,7 @@
 
                 @pl.when(chip > 0)
                 def _():
-                    l_send[h] = mm(ca[h], l_in[h], TN) + cn[h]
+                    l_send[h] = mm((ca[h], ca_low[h]), l_in[h], TN) + cn[h]
 
             @pl.when(chip > 0)
             def _():
@@ -357,7 +345,7 @@
 def last_kernel(
     heads, place_ref, hid_ref, q_ref, k_ref, v_ref, do_ref, rate_ref, bias_ref,
     t_ref, w_ref, u0_ref, p_ref, logit_ref, cum_ref, s_ref, l_ref,
-    dq_ref, dk_ref, dv_ref, lg_ref, wg_ref, small_ref,
+    dq_ref, dk_ref, dv_ref, lg_ref, x_ref,
 ):
     rows, columns = iotas()
     eye = rows == columns
@@ -448,35 +436,64 @@
     )
     logit_grad = jnp.where(columns < 2 * heads, logit_grad, 0.0)
     lg_ref[...] = logit_grad.T[: 2 * heads, :]
-    small_ref[0:1, :] = jnp.sum(decay_grad * log_decay, axis=0, keepdims=True)
-    small_ref[1:2, :] = jnp.sum(decay_logit, axis=0, keepdims=True)
-    wg_ref[...] = mm(split3(logit_grad), hid_ref[...], TN)[: 2 * heads, :]
+    x_ref[0 : 2 * heads, :] = mm(split3(logit_grad), hid_ref[...], TN)[: 2 * heads, :]
+    rate_grad = jnp.sum(decay_grad * log_decay, axis=0, keepdims=True)
+    bias_grad = jnp.sum(decay_logit, axis=0, keepdims=True)
+    for block in range(x_ref.shape[1] // LANES):
+        place_x = slice(block * LANES, (block + 1) * LANES)
+        x_ref[2 * heads : 2 * heads + 1, place_x] = rate_grad
+        x_ref[2 * heads + 1 : 2 * heads + 2, place_x] = bias_grad
+
+
+def greet_all(sizes, names):
+    barrier = pltpu.get_barrier_semaphore()
+    for size, name in zip(sizes, names):
+        place = lax.axis_index(name)
+
+        def greet(step, _, size=size, name=name, place=place):
+            peer = lax.rem(place + step, size)
+            pl.semaphore_signal(
+                barrier, inc=1, device_id={name: peer}, device_id_type=MESH
+            )
+            return 0
+
+        lax.fori_loop(1, size, greet, 0)
+    return barrier
+
+
+def each(first, last, act):
+    def body(step, _):
+        act(step)
+        return 0
+
+    lax.fori_loop(first, last, body, 0)
+
+
+def feature_copy(sizes, names, w_ref, features, send, recv, step):
+    row = lax.axis_index(names[1])
+    peer = lax.rem(row + step, sizes[1])
+    piece = features.shape[2]
+    start = pl.multiple_of(peer * piece, LANES)
+    return pltpu.make_async_remote_copy(
+        src_ref=w_ref.at[:, pl.ds(start, piece)], dst_ref=features.at[row],
+        send_sem=send.at[step], recv_sem=recv.at[step],
+        device_id={names[1]: peer}, device_id_type=MESH,
+    )
 
 
 def sum_kernel(
-    sizes, names, x_ref, lg_ref, w_ref, sum_ref, hid_ref,
-    parts, total, logits, ss, rs, ss2, rs2, lss, lrs,
+    sizes, names, heads, x_ref, lg_ref, features, hid_ref, decay_ref, beta_ref, small_ref,
+    parts, total, sums, logits, ss, rs, ss2, rs2, lss, lrs,
 ):
     count, dp_count = sizes
     ctx, dp = names
     me = lax.axis_index(ctx)
     row = lax.axis_index(dp)
-
-    barrier = pltpu.get_barrier_semaphore()
-
-    def greet(step, _):
-        peer = lax.rem(me + step, count)
-        pl.semaphore_signal(barrier, inc=1, device_id={ctx: peer}, device_id_type=MESH)
-        return 0
-
-    def greet_row(step, _):
-        peer = lax.rem(row + step, dp_count)
-        pl.semaphore_signal(barrier, inc=1, device_id={dp: peer}, device_id_type=MESH)
-        return 0
-
-    lax.fori_loop(1, count, greet, 0)
-    lax.fori_loop(1, dp_count, greet_row, 0)
-    pl.semaphore_wait(barrier, count - 1 + dp_count - 1)
+    block = parts.shape[2]
+    owners = x_ref.shape[1] // block
+
+    def columns_of(owner):
+        return pl.ds(pl.multiple_of(owner * block, LANES), block)
 
     def logit_copy(step):
         peer = lax.rem(row + step, dp_count)
@@ -486,47 +503,105 @@
         )
 
     def scatter(step):
-        peer = lax.rem(me + step, count)
-        return pltpu.make_async_remote_copy(
-            src_ref=x_ref.at[peer], dst_ref=parts.at[me], send_sem=ss.at[step],
-            recv_sem=rs.at[step], device_id={ctx: peer}, device_id_type=MESH,
+        owner = lax.rem(me + step, count)
+        return owner, lambda: pltpu.make_async_remote_copy(
+            src_ref=x_ref.at[:, columns_of(owner)], dst_ref=parts.at[me],
+            send_sem=ss.at[step], recv_sem=rs.at[step],
+            device_id={ctx: owner}, device_id_type=MESH,
         )
 
     def gather(step):
         peer = lax.rem(me + step, count)
         return pltpu.make_async_remote_copy(
-            src_ref=total, dst_ref=sum_ref.at[me], send_sem=ss2.at[step],
+            src_ref=total, dst_ref=sums.at[:, columns_of(me)], send_sem=ss2.at[step],
             recv_sem=rs2.at[step], device_id={ctx: peer}, device_id_type=MESH,
         )
 
-    def each(last, act):
-        def body(step, _):
-            act(step)
-            return 0
-
-        lax.fori_loop(1, last, body, 0)
-
-    each(count, lambda step: scatter(step).start())
-    each(dp_count, lambda step: logit_copy(step).start())
-    parts[me] = x_ref[me]
+    def from_owner(step):
+        owner = lax.rem(me - step + count, count)
+        return owner, lambda: pltpu.make_async_remote_copy(
+            src_ref=total, dst_ref=sums.at[:, columns_of(owner)], send_sem=ss2.at[step],
+            recv_sem=rs2.at[step], device_id={ctx: owner}, device_id_type=MESH,
+        )
+
+    def if_owner(owner, act):
+        if owners == count:
+            act()
+        else:
+            pl.when(owner < owners)(act)
+
+    def scatter_start(step):
+        owner, copy = scatter(step)
+        if_owner(owner, lambda: copy().start())
+
+    def scatter_done(step):
+        owner, copy = scatter(step)
+        if_owner(owner, lambda: copy().wait_send())
+
+    def gather_done(step):
+        owner, copy = from_owner(step)
+        if_owner(owner, lambda: copy().wait_recv())
+
+    each(1, count, scatter_start)
+    each(1, dp_count, lambda step: logit_copy(step).start())
     logits[row] = lg_ref[...]
-    each(count, lambda step: scatter(step).wait_recv())
-    amount = parts[0]
-    for i in range(1, count):
-        amount = amount + parts[i]
-    total[...] = amount
-    sum_ref[me] = amount
-    each(count, lambda step: gather(step).start())
-    each(dp_count, lambda step: logit_copy(step).wait_recv())
+
+    def own():
+        parts[me] = x_ref[:, columns_of(me)]
+        each(1, count, lambda step: scatter(step)[1]().wait_recv())
+        amount = parts[0]
+        for i in range(1, count):
+            amount = amount + parts[i]
+        total[...] = amount
+        sums[:, columns_of(me)] = amount
+        each(1, count, lambda step: gather(step).start())
+
+    if_owner(me, own)
+    each(1, dp_count, lambda step: logit_copy(step).wait_recv())
     hidden = None
     for d in range(dp_count):
-        term = mm(split3(logits[d]), w_ref[d], TN)
+        term = mm(split3(logits[d]), features[d].astype(bf16), TN)
         hidden = term if hidden is None else hidden + term
     hid_ref[...] = hidden.astype(bf16)
-    each(count, lambda step: gather(step).wait_recv())
-    each(count, lambda step: scatter(step).wait_send())
-    each(count, lambda step: gather(step).wait_send())
-    each(dp_count, lambda step: logit_copy(step).wait_send())
+    each(1, count, gather_done)
+    decay_ref[...] = sums[0:heads, :]
+    beta_ref[...] = sums[heads : 2 * heads, :]
+    small_ref[...] = sums[2 * heads : 2 * heads + 2, 0:LANES]
+    each(1, count, scatter_done)
+    if_owner(me, lambda: each(1, count, lambda step: gather(step).wait_send()))
+    each(1, dp_count, lambda step: logit_copy(step).wait_send())
+
+
+def whole_kernel(
+    sizes, names, heads, place_ref, hid_ref, w_ref, q_ref, k_ref, v_ref, do_ref, rate_ref,
+    bias_ref, dq_ref, dk_ref, dv_ref, hidden_ref, decay_ref, beta_ref, small_ref,
+    wide, a, b, n, t, w, u, p, s, l, logit, cum, x, lg, features, fs, fr, *rest,
+):
+    chain_rest, sum_rest = rest[:21], rest[21:]
+    barrier = greet_all(sizes, names)
+    features[lax.axis_index(names[1])] = w_ref[
+        :, pl.ds(pl.multiple_of(lax.axis_index(names[1]) * features.shape[2], LANES), features.shape[2])
+    ]
+    first_kernel(
+        heads, place_ref, hid_ref, w_ref, q_ref, k_ref, v_ref, do_ref, rate_ref, bias_ref,
+        wide, a, b, n, t, w, u, p, logit, cum,
+    )
+    pl.semaphore_wait(barrier, sizes[0] - 1 + sizes[1] - 1)
+
+    def feature(step):
+        return feature_copy(sizes, names, w_ref, features, fs, fr, step)
+
+    each(1, sizes[1], lambda step: feature(step).start())
+    chain_kernel(sizes[0], names, heads // 2, a, b, n, s, l, *chain_rest)
+    last_kernel(
+        heads, place_ref, hid_ref, q_ref, k_ref, v_ref, do_ref, rate_ref, bias_ref,
+        t, w, u, p, logit, cum, s, l, dq_ref, dk_ref, dv_ref, lg, x,
+    )
+    each(1, sizes[1], lambda step: feature(step).wait())
+    sum_kernel(
+        sizes, names, heads, x, lg, features, hidden_ref, decay_ref, beta_ref, small_ref,
+        *sum_rest,
+    )
 
 
 def on_device(
@@ -540,102 +615,71 @@
     vmem = pl.BlockSpec(memory_space=pltpu.VMEM)
     smem = pl.BlockSpec(memory_space=pltpu.SMEM)
     params = functools.partial(pltpu.CompilerParams, vmem_limit_bytes=VMEM_LIMIT)
-    both = jnp.concatenate([w_decay, w_beta], axis=1)
-    panel_w = jnp.pad(both, ((0, 0), (0, LANES - 2 * heads)))
+    weights = jnp.concatenate([w_decay.T, w_beta.T], axis=0).astype(f32)
     rate_row = jnp.pad(log_decay_rate, (0, LANES - heads))[None]
     bias_row = jnp.pad(step_bias, (0, LANES - heads))[None]
     offset = lax.axis_index("ctx") * tokens
     place = segment(doc_start, offset, tokens)
     piece = width // dp_count
-    features = lax.all_gather(both.T, "dp")
-    features = lax.dynamic_slice_in_dim(
-        features, lax.axis_index("dp") * piece, piece, axis=2
-    )
-
-    square = jax.ShapeDtypeStruct((heads, LANES, LANES), f32)
-    panel = jax.ShapeDtypeStruct((LANES, LANES), f32)
-    a, b, n, t, w, u, p, logits, cum = pl.pallas_call(
-        functools.partial(first_kernel, heads),
-        out_shape=(square,) * 7 + (panel,) * 2,
-        in_specs=[smem] + [vmem] * 8,
-        out_specs=(vmem,) * 9,
-        compiler_params=params(),
-        name="local_maps",
-    )(
-        place, hidden_in, panel_w, query_vectors, key_vectors, value_vectors,
-        out_cotangent, rate_row, bias_row,
-    )
-
     half = heads // 2
-    held = pltpu.VMEM((half, DK, DV), f32)
+    lines = -(-(2 * heads + 2) // 8) * 8
+    block = width // min(count, width // LANES)
+
+    def room(*shape, kind=f32):
+        return pltpu.VMEM(shape, kind)
+
+    square = room(heads, LANES, LANES)
+    held = room(half, LANES, LANES)
+    split_map = room(half, LANES, LANES, kind=bf16)
+    panel = room(LANES, LANES)
     dma = pltpu.SemaphoreType.DMA
-    state, adjoint = pl.pallas_call(
-        functools.partial(chain_kernel, count, names, half),
-        out_shape=(square,) * 2,
-        in_specs=[vmem] * 3,
-        out_specs=(vmem,) * 2,
-        scratch_shapes=[held] * 12
-        + [dma((3,)), dma((3,))]
-        + [dma((half,))] * 4
-        + [dma((2,)), dma((2,))],
-        compiler_params=params(collective_id=0, has_side_effects=True),
-        name="chain",
-    )(a, b, n)
-
-    query_grad, key_grad, value_grad, logit_grad, weight_grad, small = pl.pallas_call(
-        functools.partial(last_kernel, heads),
+    query_grad, key_grad, value_grad, hidden_grad, decay_sum, beta_sum, small = pl.pallas_call(
+        functools.partial(whole_kernel, sizes, names, heads),
         out_shape=(
             jax.ShapeDtypeStruct(query_vectors.shape, bf16),
             jax.ShapeDtypeStruct(key_vectors.shape, bf16),
             jax.ShapeDtypeStruct(value_vectors.shape, bf16),
-            jax.ShapeDtypeStruct((2 * heads, LANES), f32),
-            jax.ShapeDtypeStruct((2 * heads, width), f32),
+            jax.ShapeDtypeStruct((tokens, piece), bf16),
+            jax.ShapeDtypeStruct((heads, width), f32),
+            jax.ShapeDtypeStruct((heads, width), f32),
             jax.ShapeDtypeStruct((2, LANES), f32),
         ),
-        in_specs=[smem] + [vmem] * 15,
-        out_specs=(vmem,) * 6,
-        compiler_params=params(),
-        name="gradients",
-    )(
-        place, hidden_in, query_vectors, key_vectors, value_vectors, out_cotangent,
-        rate_row, bias_row, t, w, u, p, logits, cum, state, adjoint,
-    )
-
-    lines = 2 * heads * width // LANES
-    per = -(-lines // count)
-    stacked = weight_grad.reshape(lines, LANES)
-    stacked = jnp.pad(stacked, ((0, per * count - lines), (0, 0))).reshape(count, per, LANES)
-    stacked = jnp.concatenate(
-        [stacked, jnp.broadcast_to(small[None], (count, 2, LANES))], axis=1
-    )
-    summed, hidden_grad = pl.pallas_call(
-        functools.partial(sum_kernel, sizes, names),
-        out_shape=(
-            jax.ShapeDtypeStruct(stacked.shape, f32),
-            jax.ShapeDtypeStruct((tokens, piece), bf16),
-        ),
-        in_specs=[vmem] * 3,
-        out_specs=(vmem,) * 2,
-        scratch_shapes=[
-            pltpu.VMEM(stacked.shape, f32),
-            pltpu.VMEM(stacked.shape[1:], f32),
-            pltpu.VMEM((dp_count,) + logit_grad.shape, f32),
+        in_specs=[smem] + [vmem] * 8,
+        out_specs=(vmem,) * 7,
+        scratch_shapes=[room(LANES, width)]
+        + [square] * 9
+        + [panel] * 2
+        + [room(lines, width), room(2 * heads, LANES), room(dp_count, 2 * heads, piece)]
+        + [dma((dp_count,))] * 2
+        + [held] * 9
+        + [split_map] * 2
+        + [held] * 2
+        + [dma((3,))] * 2
+        + [dma((half,))] * 4
+        + [dma((2,))] * 2
+        + [
+            room(count, lines, block),
+            room(lines, block),
+            room(lines, width),
+            room(dp_count, 2 * heads, LANES),
         ]
         + [dma((count,))] * 4
         + [dma((dp_count,))] * 2,
-        compiler_params=params(collective_id=1, has_side_effects=True),
-        name="totals",
-    )(stacked, logit_grad, features)
-    weights = summed[:, :per].reshape(per * count, LANES)[:lines].reshape(2 * heads, width).T
+        compiler_params=params(collective_id=0, has_side_effects=True),
+        name="layer_backward",
+    )(
+        place, hidden_in, weights, query_vectors, key_vectors, value_vectors,
+        out_cotangent, rate_row, bias_row,
+    )
     return (
         query_grad,
         key_grad,
         value_grad,
         hidden_grad,
-        weights[:, :heads],
-        weights[:, heads:],
-        summed[0, per, :heads],
-        summed[0, per + 1, :heads],
+        decay_sum.T,
+        beta_sum.T,
+        small[0, :heads],
+        small[1, :heads],
     )
 
 

time: 97.5 us -> 82.7 us (0.85)
  Pallas kernels: 80 us -> 71.4 us
  blocking collectives: 5.85 us -> 0 us
  local copies, waits for them, and re-layouts: 9.15 us -> 8.04 us
    pallas_call x4 -> x1, Pallas kernels: 80 us -> 71.4 us  [on_device(): pl.pallas_call(functools.partial(whole_kernel, sizes, names, heads), out_...]
    all_gather x1 -> x0, blocking collectives: 5.85 us -> none  [on_device(): features = lax.all_gather(both.T, 'dp')]
    unnamed x16 -> x20, local copies, waits for them, and re-layouts: 3.95 us -> 6.33 us
    slice x2 -> x0, local copies, waits for them, and re-layouts: 1.57 us -> none  [the longest x1 0.92 us: on_device(): summed[:, :per].reshape(per * count, LANES)[:lines]]
    convert_element_type x0 -> x1, other arithmetic: none -> 1.42 us  [on_device(): weights = jnp.concatenate([w_decay.T, w_beta.T], axis=0).astype(f32)]
where the time goes in v2:
time: 82.7 us; the launch traced here: 82.2 us
  Pallas kernels  71.4 us (86%)
  local copies, waits for them, and re-layouts  8.04 us (10%)
  other arithmetic  1.42 us (2%)
  between operations  1.34 us (2%)
    pallas_call x1, Pallas kernels, on_device(): pl.pallas_call(functools.partial(whole_kernel, sizes, names, heads), out_...  71.4 us
    unnamed x20, local copies, waits for them, and re-layouts  6.33 us

profile of v2, /device:TPU:0, one launch (start us, length us, event | category | flops | bytes accessed | tf_op | source)
XLA Modules:
  0.0 82.2 jit_solution(18436781887428393866)
XLA Ops:
  0.6 0.0 copy-start.5
  1.3 1.2 %pad_bitcast_fusion = (f32[1,128]{1,0:T(1,128)}, f32[1,128]{1,0:T(1,128)}) fusion(f32[8]{0:T(128)} %param.18, f32[8]{0:T(128)} %param.17), kind=kLoop, calls=%fused_computation.3 | loop fusion | bytes 1088 | tf_op jit(solution)/shard_map/broadcast_in_dim | solution.py:620
  2.5 0.0 copy-done.5
  2.5 1.4 %maximum_convert_fusion.w_ref = f32[16,2048]{1,0:T(8,128)} fusion(bf16[8,2048]{1,0:T(8,128)(2,1)S(1)} %bitcast.16, bf16[8,2048]{1,0:T(8,128)(2,1)} %bitcast.17), kind=kLoop, calls=%fused_computation | loop fusion | flops 131072 | bytes 196608 | tf_op jit(solution)/shard_map/convert_element_type | solution.py:618
  3.9 71.4 %layer_backward.1 = (bf16[128,512]{1,0:T(8,128)(2,1)}, bf16[128,512]{1,0:T(8,128)(2,1)}, bf16[128,1024]{1,0:T(8,128)(2,1)}, bf16[128,1024]{1,0:T(8,128)(2,1)}, f...) custom-call(s32[1]{0:T(128)S(6)} %select_n.4.place_ref, bf16[128,2048]{1,0:T(8,128)(2,1)} %hid_ref.1, ...), custom_call_target="tpu_custom_call" | custom-call | tf_op jit(solution)/shard_map/layer_backward/pallas_call | solution.py:636
  75.4 0.0 copy-start.6
  75.4 0.6 copy-done.6
  76.0 0.5 slice_bitcast_fusion
  76.5 0.0 copy-start.2
  76.5 0.0 copy-start.1
  76.5 1.6 %copy.25 = bf16[128,512]{1,0:T(8,128)(2,1)} copy(bf16[128,512]{1,0:T(8,128)(2,1)} %get-tuple-element.34) | data formatting | bytes 262144
  78.2 0.0 copy-done.2
  78.2 0.7 copy.26
  78.8 0.0 copy-done.1
  78.8 0.0 copy-start
  78.8 0.7 copy.27
  79.5 0.3 copy-done
  79.9 0.0 copy-start.4
  79.9 0.7 copy.28
  80.6 0.2 copy-done.4
  80.7 0.0 copy-start.3
  80.7 0.6 copy.29
  81.4 0.2 copy-done.3
  81.6 0.6 copy.30
Async XLA Ops:
  0.6 1.9 %copy-start.5 = (bf16[2048,8]{0,1:T(8,128)(2,1)S(1)}, bf16[2048,8]{0,1:T(8,128)(2,1)}, u32[]{:S(2)}) copy-start(bf16[2048,8]{0,1:T(8,128)(2,1)} %param.16) | copy-start | bytes 98308
  75.4 0.7 copy-start.6
  76.5 1.6 %copy-start.2 = (bf16[128,512]{1,0:T(8,128)(2,1)S(1)}, bf16[128,512]{1,0:T(8,128)(2,1)}, u32[]{:S(2)}) copy-start(bf16[128,512]{1,0:T(8,128)(2,1)} %get-tuple-element.35) | copy-start | bytes 393220
  76.5 2.3 %copy-start.1 = (bf16[128,1024]{1,0:T(8,128)(2,1)S(1)}, bf16[128,1024]{1,0:T(8,128)(2,1)}, u32[]{:S(2)}) copy-start(bf16[128,1024]{1,0:T(8,128)(2,1)} %get-tuple-element.36) | copy-start | bytes 786436
  78.8 1.0 %copy-start = (bf16[128,1024]{1,0:T(8,128)(2,1)S(1)}, bf16[128,1024]{1,0:T(8,128)(2,1)}, u32[]{:S(2)}) copy-start(bf16[128,1024]{1,0:T(8,128)(2,1)} %get-tuple-element.37) | copy-start | bytes 786436
  79.9 0.9 %copy-start.4 = (f32[8,2048]{1,0:T(8,128)S(1)}, f32[8,2048]{1,0:T(8,128)}, u32[]{:S(2)}) copy-start(f32[8,2048]{1,0:T(8,128)} %get-tuple-element.19) | copy-start | bytes 196612
  80.7 0.9 %copy-start.3 = (f32[8,2048]{1,0:T(8,128)S(1)}, f32[8,2048]{1,0:T(8,128)}, u32[]{:S(2)}) copy-start(f32[8,2048]{1,0:T(8,128)} %get-tuple-element.20) | copy-start | bytes 196612

commit v3 on v2

--- a/solution.py
+++ b/solution.py
@@ -10,6 +10,7 @@
 DK = 128
 DV = 128
 LANES = 128
+CHUNKS = 2
 norm_epsilon = 1e-06
 
 MESH = pl.DeviceIdType.MESH
@@ -108,14 +109,13 @@
 
 
 def first_kernel(
-    heads, place_ref, hid_ref, w_ref, q_ref, k_ref, v_ref, do_ref, rate_ref, bias_ref,
+    heads, place, hid_ref, w_ref, q_ref, k_ref, v_ref, do_ref, rate_ref, bias_ref,
     wide_ref, a_ref, b_ref, n_ref, t_ref, w_out_ref, u_ref, p_ref, logit_ref, cum_ref,
 ):
     rows, columns = iotas()
     eye = rows == columns
     lower = rows >= columns
     strict = rows > columns
-    place = place_ref[0]
     wide_ref[...] = jnp.zeros_like(wide_ref)
     wide_ref[0 : 2 * heads, :] = w_ref[...]
     logits = one_pass(hid_ref[...], wide_ref[...].astype(bf16), NT)
@@ -172,15 +172,15 @@
         u_ref[h] = u
         weight = rk * to_last
         a_ref[h] = last_carry * eye_f - mm(kb, w * weight, TN)
-        b_ref[h] = mm(kb, u * weight, TN)
+        b_ref[h] = mm(u * weight, kb, TN)
         reach = (carry * rq) * qb.astype(f32) - mm(p_ref[h], w)
-        n_ref[h] = mm(reach, dob, TN)
+        n_ref[h] = mm(dob, reach, TN)
 
 
 def chain_kernel(
     count, names, half, a_ref, b_ref, n_ref, s_ref, l_ref,
     pa, pb, pn, s_in, l_in, s_send, l_send, s_give, l_give, ca, ca_low, cb, cn,
-    swap_send, swap_recv, s_ss, s_rs, l_ss, l_rs, g_send, g_recv,
+    swap_send, swap_recv, s_ss, s_rs, l_ss, l_rs, gs_send, gs_recv, gl_send, gl_recv,
 ):
     ctx, dp = names
     me = lax.axis_index(ctx)
@@ -211,8 +211,8 @@
             later = split(second_a(h))
             earlier = split(first_a(h))
             ca[h], ca_low[h] = split(mm(later, earlier))
-            cb[h] = mm(later, first_b(h)) + second_b(h)
-            cn[h] = mm(earlier, second_n(h), TN) + first_n(h)
+            cb[h] = mm(first_b(h), later, NT) + second_b(h)
+            cn[h] = mm(second_n(h), earlier) + first_n(h)
 
     own = [lambda h, r=r: r[mine + h] for r in (a_ref, b_ref, n_ref)]
     other = [lambda h, r=r: r[h] for r in (pa, pb, pn)]
@@ -225,125 +225,149 @@
     def _():
         compose(*other, *own)
 
-    def s_copy(h):
+    rows = DV // CHUNKS
+    units = half * CHUNKS
+
+    def part(ref, i, head=None):
+        head = i // CHUNKS if head is None else head
+        return ref.at[head, pl.ds((i % CHUNKS) * rows, rows)]
+
+    def s_copy(i):
         return pltpu.make_async_remote_copy(
-            src_ref=s_send.at[h], dst_ref=s_in.at[h], send_sem=s_ss.at[h],
-            recv_sem=s_rs.at[h], device_id=at(me + 2), device_id_type=MESH,
-        )
-
-    def l_copy(h):
+            src_ref=part(s_send, i), dst_ref=part(s_in, i), send_sem=s_ss.at[i],
+            recv_sem=s_rs.at[i], device_id=at(me + 2), device_id_type=MESH,
+        )
+
+    def l_copy(i):
         return pltpu.make_async_remote_copy(
-            src_ref=l_send.at[h], dst_ref=l_in.at[h], send_sem=l_ss.at[h],
-            recv_sem=l_rs.at[h], device_id=at(me - 2), device_id_type=MESH,
-        )
-
-    def forward():
-        for h in range(half):
-
-            @pl.when(chip == 0)
+            src_ref=part(l_send, i), dst_ref=part(l_in, i), send_sem=l_ss.at[i],
+            recv_sem=l_rs.at[i], device_id=at(me - 2), device_id_type=MESH,
+        )
+
+    def give(source, target, i, send, recv):
+        return pltpu.make_async_remote_copy(
+            src_ref=part(source, i), dst_ref=part(target, i, mine + i // CHUNKS),
+            send_sem=send.at[i], recv_sem=recv.at[i],
+            device_id=at(mate), device_id_type=MESH,
+        )
+
+    def forward(i):
+        h = i // CHUNKS
+
+        @pl.when(chip == 0)
+        def _():
+            part(s_in, i)[...] = jnp.zeros((rows, DK), f32)
+            part(s_send, i)[...] = part(cb, i)[...]
+
+        @pl.when(chip > 0)
+        def _():
+            s_copy(i).wait_recv()
+
+            @pl.when(chip < chips - 1)
             def _():
-                s_in[h] = jnp.zeros((DK, DV), f32)
-                s_send[h] = cb[h]
+                step = mm(part(s_in, i)[...], (ca[h], ca_low[h]), NT)
+                part(s_send, i)[...] = step + part(cb, i)[...]
+
+        @pl.when(chip < chips - 1)
+        def _():
+            s_copy(i).start()
+
+    def backward(i):
+        h = i // CHUNKS
+
+        @pl.when(chip == chips - 1)
+        def _():
+            part(l_in, i)[...] = jnp.zeros((rows, DK), f32)
+            part(l_send, i)[...] = part(cn, i)[...]
+
+        @pl.when(chip < chips - 1)
+        def _():
+            l_copy(i).wait_recv()
 
             @pl.when(chip > 0)
             def _():
-                s_copy(h).wait_recv()
-
-                @pl.when(chip < chips - 1)
-                def _():
-                    s_send[h] = mm((ca[h], ca_low[h]), s_in[h]) + cb[h]
-
-            @pl.when(chip < chips - 1)
-            def _():
-                s_copy(h).start()
-
-    def backward():
-        for h in range(half):
-
-            @pl.when(chip == chips - 1)
-            def _():
-                l_in[h] = jnp.zeros((DK, DV), f32)
-                l_send[h] = cn[h]
-
-            @pl.when(chip < chips - 1)
-            def _():
-                l_copy(h).wait_recv()
-
-                @pl.when(chip > 0)
-                def _():
-                    l_send[h] = mm((ca[h], ca_low[h]), l_in[h], TN) + cn[h]
-
-            @pl.when(chip > 0)
-            def _():
-                l_copy(h).start()
-
-    def give(source, target, i):
-        return pltpu.make_async_remote_copy(
-            src_ref=source, dst_ref=target.at[pl.ds(mine, half)], send_sem=g_send.at[i],
-            recv_sem=g_recv.at[i], device_id=at(mate), device_id_type=MESH,
-        )
-
-    def finish_s():
+                step = mm(part(l_in, i)[...], (ca[h], ca_low[h]))
+                part(l_send, i)[...] = step + part(cn, i)[...]
+
+        @pl.when(chip > 0)
+        def _():
+            l_copy(i).start()
+
+    def finish_s(i):
+        h = i // CHUNKS
+        own_part = part(s_ref, i, mine + h)
+
         @pl.when(core == 0)
         def _():
-            for h in range(half):
-                s_ref[mine + h] = s_in[h]
-                s_give[h] = mm(a_ref[mine + h], s_in[h]) + b_ref[mine + h]
+            state = part(s_in, i)[...]
+            own_part[...] = state
+            step = mm(state, a_ref[mine + h], NT)
+            part(s_give, i)[...] = step + part(b_ref, i, mine + h)[...]
 
         @pl.when(core == 1)
         def _():
-            for h in range(half):
-                s_ref[mine + h] = mm(pa[h], s_in[h]) + pb[h]
-                s_give[h] = s_in[h]
-
-        give(s_give, s_ref, 0).start()
-
-    def finish_l():
+            state = part(s_in, i)[...]
+            own_part[...] = mm(state, pa[h], NT) + part(pb, i)[...]
+            part(s_give, i)[...] = state
+
+        give(s_give, s_ref, i, gs_send, gs_recv).start()
+
+    def finish_l(i):
+        h = i // CHUNKS
+        own_part = part(l_ref, i, mine + h)
+
         @pl.when(core == 1)
         def _():
-            for h in range(half):
-                l_ref[mine + h] = l_in[h]
-                l_give[h] = mm(a_ref[mine + h], l_in[h], TN) + n_ref[mine + h]
+            adjoint = part(l_in, i)[...]
+            own_part[...] = adjoint
+            step = mm(adjoint, a_ref[mine + h])
+            part(l_give, i)[...] = step + part(n_ref, i, mine + h)[...]
 
         @pl.when(core == 0)
         def _():
-            for h in range(half):
-                l_ref[mine + h] = mm(pa[h], l_in[h], TN) + pn[h]
-                l_give[h] = l_in[h]
-
-        give(l_give, l_ref, 1).start()
+            adjoint = part(l_in, i)[...]
+            own_part[...] = mm(adjoint, pa[h]) + part(pn, i)[...]
+            part(l_give, i)[...] = adjoint
+
+        give(l_give, l_ref, i, gl_send, gl_recv).start()
 
     @pl.when(2 * chip < chips)
     def _():
-        forward()
-        finish_s()
-        backward()
-        finish_l()
+        for i in range(units):
+            forward(i)
+        for i in range(units):
+            finish_s(i)
+        for i in range(units):
+            backward(i)
+            finish_l(i)
 
     @pl.when(2 * chip >= chips)
     def _():
-        backward()
-        finish_l()
-        forward()
-        finish_s()
-
-    for h in range(half):
+        for i in range(units):
+            backward(i)
+        for i in range(units):
+            finish_l(i)
+        for i in range(units):
+            forward(i)
+            finish_s(i)
+
+    for i in range(units):
 
         @pl.when(chip < chips - 1)
         def _():
-            s_copy(h).wait_send()
+            s_copy(i).wait_send()
 
         @pl.when(chip > 0)
         def _():
-            l_copy(h).wait_send()
-
-    for i, (source, target) in enumerate(((s_give, s_ref), (l_give, l_ref))):
-        give(source, target, i).wait_send()
-        give(source, target, i).wait_recv()
+            l_copy(i).wait_send()
+
+    for i in range(units):
+        give(s_give, s_ref, i, gs_send, gs_recv).wait()
+        give(l_give, l_ref, i, gl_send, gl_recv).wait()
 
 
 def last_kernel(
-    heads, place_ref, hid_ref, q_ref, k_ref, v_ref, do_ref, rate_ref, bias_ref,
+    heads, place, hid_ref, q_ref, k_ref, v_ref, do_ref, rate_ref, bias_ref,
     t_ref, w_ref, u0_ref, p_ref, logit_ref, cum_ref, s_ref, l_ref,
     dq_ref, dk_ref, dv_ref, lg_ref, x_ref,
 ):
@@ -351,7 +375,6 @@
     eye = rows == columns
     lower = rows >= columns
     strict = rows > columns
-    place = place_ref[0]
     logits = logit_ref[...]
     cum = cum_ref[...]
     beta_all = sigmoid(logits)
@@ -381,20 +404,20 @@
         beta = beta_all[:, heads + h : heads + h + 1]
         state_f, adjoint_f = s_ref[h], l_ref[h]
         state, adjoint = split(state_f), split(adjoint_f)
-        key_state = mm(kb, state) * rk
-        query_state = mm(qb, state) * rq
-        updates_f = u0_ref[h] - mm(w_ref[h], state)
+        key_state = mm(kb, state, NT) * rk
+        query_state = mm(qb, state, NT) * rq
+        updates_f = u0_ref[h] - mm(w_ref[h], state, NT)
         updates = split(updates_f)
-        update_grad = mm(p_ref[h], dob, TN) + mm(kb, adjoint) * (rk * to_last)
+        update_grad = mm(p_ref[h], dob, TN) + mm(kb, adjoint, NT) * (rk * to_last)
         score_grad = mm(dob, updates, NT) * decay
         z_f = mm(t_ref[h], update_grad, TN)
         z = split(z_f)
         dv_ref[:, h * DV : (h + 1) * DV] = (beta * z_f).astype(bf16)
         coupling_grad = jnp.where(strict, -mm(z, updates, NT), 0.0) * decay
         gram_grad = coupling_grad * beta
-        last_keys = mm(updates, adjoint, NT)
-        q_hat_grad += carry * mm(dob, state, NT)
-        k_hat_grad += last_keys * to_last - (beta * carry) * mm(z, state, NT)
+        last_keys = mm(updates, adjoint)
+        q_hat_grad += carry * mm(dob, state)
+        k_hat_grad += last_keys * to_last - (beta * carry) * mm(z, state)
         score_sum += score_grad
         gram_sum += gram_grad
         value_f = vb.astype(f32)
@@ -573,17 +596,30 @@
 
 
 def whole_kernel(
-    sizes, names, heads, place_ref, hid_ref, w_ref, q_ref, k_ref, v_ref, do_ref, rate_ref,
-    bias_ref, dq_ref, dk_ref, dv_ref, hidden_ref, decay_ref, beta_ref, small_ref,
+    sizes, names, heads, doc_ref, rate_in, bias_in, hid_ref, wd_ref, wb_ref, q_ref, k_ref,
+    v_ref, do_ref, dq_ref, dk_ref, dv_ref, hidden_ref, decay_ref, beta_ref, small_ref,
+    w_ref, rate_ref, bias_ref,
     wide, a, b, n, t, w, u, p, s, l, logit, cum, x, lg, features, fs, fr, *rest,
 ):
-    chain_rest, sum_rest = rest[:21], rest[21:]
+    tokens = hid_ref.shape[0]
+    place = segment(doc_ref[0], lax.axis_index(names[0]) * tokens, tokens)
+    w_ref[0:heads, :] = wd_ref[...].astype(f32)
+    w_ref[heads : 2 * heads, :] = wb_ref[...].astype(f32)
+    lane = lax.broadcasted_iota(jnp.int32, (1, LANES), 1)
+    rate_row = jnp.zeros((1, LANES), f32)
+    bias_row = jnp.zeros((1, LANES), f32)
+    for h in range(heads):
+        rate_row = jnp.where(lane == h, rate_in[h], rate_row)
+        bias_row = jnp.where(lane == h, bias_in[h], bias_row)
+    rate_ref[...] = rate_row
+    bias_ref[...] = bias_row
+    chain_rest, sum_rest = rest[:23], rest[23:]
     barrier = greet_all(sizes, names)
     features[lax.axis_index(names[1])] = w_ref[
         :, pl.ds(pl.multiple_of(lax.axis_index(names[1]) * features.shape[2], LANES), features.shape[2])
     ]
     first_kernel(
-        heads, place_ref, hid_ref, w_ref, q_ref, k_ref, v_ref, do_ref, rate_ref, bias_ref,
+        heads, place, hid_ref, w_ref, q_ref, k_ref, v_ref, do_ref, rate_ref, bias_ref,
         wide, a, b, n, t, w, u, p, logit, cum,
     )
     pl.semaphore_wait(barrier, sizes[0] - 1 + sizes[1] - 1)
@@ -594,7 +630,7 @@
     each(1, sizes[1], lambda step: feature(step).start())
     chain_kernel(sizes[0], names, heads // 2, a, b, n, s, l, *chain_rest)
     last_kernel(
-        heads, place_ref, hid_ref, q_ref, k_ref, v_ref, do_ref, rate_ref, bias_ref,
+        heads, place, hid_ref, q_ref, k_ref, v_ref, do_ref, rate_ref, bias_ref,
         t, w, u, p, logit, cum, s, l, dq_ref, dk_ref, dv_ref, lg, x,
     )
     each(1, sizes[1], lambda step: feature(step).wait())
@@ -602,6 +638,21 @@
         sizes, names, heads, x, lg, features, hidden_ref, decay_ref, beta_ref, small_ref,
         *sum_rest,
     )
+
+
+def move_kernel(heads, *refs):
+    sources, small_ref, targets = refs[:6], refs[6], refs[7:13]
+    rate_ref, bias_ref, sems = refs[13:]
+    copies = [
+        pltpu.make_async_copy(source, target, sems.at[i])
+        for i, (source, target) in enumerate(zip(sources, targets))
+    ]
+    for copy in copies:
+        copy.start()
+    rate_ref[...] = small_ref[0:1, 0:heads]
+    bias_ref[...] = small_ref[1:2, 0:heads]
+    for copy in copies:
+        copy.wait()
 
 
 def on_device(
@@ -615,11 +666,6 @@
     vmem = pl.BlockSpec(memory_space=pltpu.VMEM)
     smem = pl.BlockSpec(memory_space=pltpu.SMEM)
     params = functools.partial(pltpu.CompilerParams, vmem_limit_bytes=VMEM_LIMIT)
-    weights = jnp.concatenate([w_decay.T, w_beta.T], axis=0).astype(f32)
-    rate_row = jnp.pad(log_decay_rate, (0, LANES - heads))[None]
-    bias_row = jnp.pad(step_bias, (0, LANES - heads))[None]
-    offset = lax.axis_index("ctx") * tokens
-    place = segment(doc_start, offset, tokens)
     piece = width // dp_count
     half = heads // 2
     lines = -(-(2 * heads + 2) // 8) * 8
@@ -644,9 +690,10 @@
             jax.ShapeDtypeStruct((heads, width), f32),
             jax.ShapeDtypeStruct((2, LANES), f32),
         ),
-        in_specs=[smem] + [vmem] * 8,
+        in_specs=[smem] * 3 + [vmem] * 7,
         out_specs=(vmem,) * 7,
-        scratch_shapes=[room(LANES, width)]
+        scratch_shapes=[room(2 * heads, width), room(1, LANES), room(1, LANES)]
+        + [room(LANES, width)]
         + [square] * 9
         + [panel] * 2
         + [room(lines, width), room(2 * heads, LANES), room(dp_count, 2 * heads, piece)]
@@ -655,8 +702,7 @@
         + [split_map] * 2
         + [held] * 2
         + [dma((3,))] * 2
-        + [dma((half,))] * 4
-        + [dma((2,))] * 2
+        + [dma((half * CHUNKS,))] * 8
         + [
             room(count, lines, block),
             room(lines, block),
@@ -668,19 +714,22 @@
         compiler_params=params(collective_id=0, has_side_effects=True),
         name="layer_backward",
     )(
-        place, hidden_in, weights, query_vectors, key_vectors, value_vectors,
-        out_cotangent, rate_row, bias_row,
-    )
-    return (
-        query_grad,
-        key_grad,
-        value_grad,
-        hidden_grad,
-        decay_sum.T,
-        beta_sum.T,
-        small[0, :heads],
-        small[1, :heads],
-    )
+        doc_start, log_decay_rate, step_bias, hidden_in, w_decay.T, w_beta.T,
+        query_vectors, key_vectors, value_vectors, out_cotangent,
+    )
+    moved = (query_grad, key_grad, value_grad, hidden_grad, decay_sum, beta_sum)
+    anywhere = pl.BlockSpec(memory_space=pl.ANY)
+    row = jax.ShapeDtypeStruct((1, heads), f32)
+    *moved, rate_grad, bias_grad = pl.pallas_call(
+        functools.partial(move_kernel, heads),
+        out_shape=tuple(jax.ShapeDtypeStruct(m.shape, m.dtype) for m in moved) + (row, row),
+        in_specs=[anywhere] * 6 + [vmem],
+        out_specs=(anywhere,) * 6 + (vmem,) * 2,
+        scratch_shapes=[dma((6,))],
+        compiler_params=params(),
+        name="results",
+    )(*moved, small)
+    return (*moved[:4], moved[4].T, moved[5].T, rate_grad[0], bias_grad[0])
 
 
 def solution(mesh):

time: 82.7 us -> 102 us (1.23)
  Pallas kernels: 71.4 us -> 100 us
  local copies, waits for them, and re-layouts: 8.04 us -> 0 us
  other arithmetic: 1.42 us -> 0 us
    pallas_call x0 -> x1, Pallas kernels: none -> 30.1 us  [on_device(): pl.pallas_call(functools.partial(move_kernel, heads), out_shape=tuple((ja...]
    unnamed x20 -> x0, local copies, waits for them, and re-layouts: 6.33 us -> none
    pallas_call x1, Pallas kernels: 71.4 us -> 69.9 us  [on_device(): pl.pallas_call(functools.partial(whole_kernel, sizes, names, heads), out_...]
    convert_element_type x1 -> x0, other arithmetic: 1.42 us -> none  [on_device(): weights = jnp.concatenate([w_decay.T, w_beta.T], axis=0).astype(f32)]
    broadcast_in_dim x1 -> x0, local copies, waits for them, and re-layouts: 1.19 us -> none  [on_device(): bias_row = jnp.pad(step_bias, (0, LANES - heads))[None]]
where the time goes in v3:
time: 102 us; the launch traced here: 101 us
  Pallas kernels  100 us (98%)
  between operations  1.45 us (1%)
    pallas_call x1, Pallas kernels, on_device(): pl.pallas_call(functools.partial(whole_kernel, sizes, names, heads), out_...  69.9 us
    pallas_call x1, Pallas kernels, on_device(): pl.pallas_call(functools.partial(move_kernel, heads), out_shape=tuple((ja...  30.1 us

profile of v3, /device:TPU:0, one launch (start us, length us, event | category | flops | bytes accessed | tf_op | source)
XLA Modules:
  0.0 101.5 jit_solution(16857406473296380909)
XLA Ops:
  1.3 69.9 %layer_backward.1 = (bf16[128,512]{1,0:T(8,128)(2,1)}, bf16[128,512]{1,0:T(8,128)(2,1)}, bf16[128,1024]{1,0:T(8,128)(2,1)}, bf16[128,1024]{1,0:T(8,128)(2,1)}, f...) custom-call(s32[1]{0:T(128)S(6)} %copy.18.doc_ref, f32[8]{0:T(128)} %rate_in.1, f32[8]{0:T(128)} %bias_in.1, ...), custom_call_target="tpu_custom_call" | custom-call | tf_op jit(solution)/shard_map/layer_backward/pallas_call | solution.py:682
  71.2 30.1 %results.1 = (bf16[128,512]{1,0:T(8,128)(2,1)}, bf16[128,512]{1,0:T(8,128)(2,1)}, bf16[128,1024]{1,0:T(8,128)(2,1)}, bf16[128,1024]{1,0:T(8,128)(2,1)}, f32[8,20...) custom-call(bf16[128,512]{1,0:T(8,128)(2,1)} %get-tuple-element.23.refs_0_, ...), custom_call_target="tpu_custom_call" | custom-call | tf_op jit(solution)/shard_map/results/pallas_call | solution.py:723

commit v4 on v3

--- a/solution.py
+++ b/solution.py
@@ -642,17 +642,11 @@
 
 def move_kernel(heads, *refs):
     sources, small_ref, targets = refs[:6], refs[6], refs[7:13]
-    rate_ref, bias_ref, sems = refs[13:]
-    copies = [
-        pltpu.make_async_copy(source, target, sems.at[i])
-        for i, (source, target) in enumerate(zip(sources, targets))
-    ]
-    for copy in copies:
-        copy.start()
+    rate_ref, bias_ref = refs[13:]
+    for source, target in zip(sources, targets):
+        target[...] = source[...]
     rate_ref[...] = small_ref[0:1, 0:heads]
     bias_ref[...] = small_ref[1:2, 0:heads]
-    for copy in copies:
-        copy.wait()
 
 
 def on_device(
@@ -718,14 +712,12 @@
         query_vectors, key_vectors, value_vectors, out_cotangent,
     )
     moved = (query_grad, key_grad, value_grad, hidden_grad, decay_sum, beta_sum)
-    anywhere = pl.BlockSpec(memory_space=pl.ANY)
     row = jax.ShapeDtypeStruct((1, heads), f32)
     *moved, rate_grad, bias_grad = pl.pallas_call(
         functools.partial(move_kernel, heads),
         out_shape=tuple(jax.ShapeDtypeStruct(m.shape, m.dtype) for m in moved) + (row, row),
-        in_specs=[anywhere] * 6 + [vmem],
-        out_specs=(anywhere,) * 6 + (vmem,) * 2,
-        scratch_shapes=[dma((6,))],
+        in_specs=[vmem] * 7,
+        out_specs=(vmem,) * 8,
         compiler_params=params(),
         name="results",
     )(*moved, small)

time: 102 us -> 73.6 us (0.72)
  Pallas kernels: 100 us -> 72 us
    pallas_call x1, Pallas kernels: 30.1 us -> 2.13 us  [on_device(): pl.pallas_call(functools.partial(move_kernel, heads), out_shape=tuple((ja...]
where the time goes in v4:
time: 73.6 us; the launch traced here: 73.4 us
  Pallas kernels  72 us (98%)
  between operations  1.39 us (2%)
    pallas_call x1, Pallas kernels, on_device(): pl.pallas_call(functools.partial(whole_kernel, sizes, names, heads), out_...  69.9 us
    pallas_call x1, Pallas kernels, on_device(): pl.pallas_call(functools.partial(move_kernel, heads), out_shape=tuple((ja...  2.13 us

profile of v4, /device:TPU:0, one launch (start us, length us, event | category | flops | bytes accessed | tf_op | source)
XLA Modules:
  0.0 73.4 jit_solution(3442254701186065942)
XLA Ops:
  1.3 69.9 %layer_backward.1 = (bf16[128,512]{1,0:T(8,128)(2,1)}, bf16[128,512]{1,0:T(8,128)(2,1)}, bf16[128,1024]{1,0:T(8,128)(2,1)}, bf16[128,1024]{1,0:T(8,128)(2,1)}, f...) custom-call(s32[1]{0:T(128)S(6)} %copy.18.doc_ref, f32[8]{0:T(128)} %rate_in.1, f32[8]{0:T(128)} %bias_in.1, ...), custom_call_target="tpu_custom_call" | custom-call | tf_op jit(solution)/shard_map/layer_backward/pallas_call | solution.py:676
  71.2 2.1 %results.1 = (bf16[128,512]{1,0:T(8,128)(2,1)}, bf16[128,512]{1,0:T(8,128)(2,1)}, bf16[128,1024]{1,0:T(8,128)(2,1)}, bf16[128,1024]{1,0:T(8,128)(2,1)}, f32[8,20...) custom-call(bf16[128,512]{1,0:T(8,128)(2,1)} %get-tuple-element.23.refs_0_, ...), custom_call_target="tpu_custom_call" | custom-call | tf_op jit(solution)/shard_map/results/pallas_call | solution.py:716
